TPU v7x, 32 devices: a whole 2x2x4 slice. The times are simulated.
32 devices in a mesh: shard: 4 (over y, x), rep: 8 (over z, core).
Axes of the slice: x: 2, y: 2, z: 4, core: 2. Of those that a mesh axis runs over, the one named last changes fastest.
Arguments:
- latents: bfloat16 [96, 256, 384], P(('shard', 'rep')), may hold values from -6 to 6
- cotangent: bfloat16 [96, 256, 384], P(('shard', 'rep')), may hold values from -6 to 6
- timesteps: int32 [96], P(('shard', 'rep')), may hold values from 0 to 999
- labels: int32 [96], P(('shard', 'rep')), may hold values from 0 to 1000
- time_table: float32 [1000, 384], replicated, may hold values from -6 to 6
- class_table: float32 [1001, 384], replicated, may hold values from -6 to 6
- w_ada: bfloat16 [384, 2304], P('shard'), may hold values from -0.3125 to 0.3125
- b_ada: bfloat16 [2304], P('shard'), may hold values from -3 to 3
- w_qkv: bfloat16 [384, 1152], P('shard'), may hold values from -1.5 to 1.5, as said below
- b_qv: bfloat16 [768], P('shard'), may hold values from -3 to 3
- w_out: bfloat16 [384, 384], P('shard'), may hold values from -1.25 to 1.25
- b_out: bfloat16 [384], P('shard'), may hold values from -6 to 6
- w_up: bfloat16 [384, 1536], P('shard'), may hold values from -0.3125 to 0.3125
- b_up: bfloat16 [1536], P('shard'), may hold values from -3 to 3
- w_down: bfloat16 [1536, 384], P('shard'), may hold values from -0.15625 to 0.15625
- b_down: bfloat16 [384], P('shard'), may hold values from -6 to 6
Outputs:
- block_out: float32 [96, 256, 384], P(('shard', 'rep'))
- input_grad: float32 [96, 256, 384], P(('shard', 'rep'))
- cond_grad: float32 [96, 384], P(('shard', 'rep'))
- grad_w_ada: float32 [384, 2304], P('shard')
- grad_b_ada: float32 [2304], P('shard')
- grad_w_qkv: float32 [384, 1152], P('shard')
- grad_b_qv: float32 [768], P('shard')
- grad_w_out: float32 [384, 384], P('shard')
- grad_b_out: float32 [384], P('shard')
- grad_w_up: float32 [384, 1536], P('shard')
- grad_b_up: float32 [1536], P('shard')
- grad_w_down: float32 [1536, 384], P('shard')
- grad_b_down: float32 [384], P('shard')
Inputs may be any that keep to these rules, and one draw needn't show every extreme that they name: `w_qkv`: entries of the projections are independent.
All inputs are finite; a program needn't handle non-finite values.
Results may differ from a plain program's by a relative error of at most 0.011.
The roundings to bfloat16 on the way count: a program that leaves them out, or rounds other values in their place, can miss the bound.
Values may be sent and summed in bfloat16 or wider, within the bound.
A program may use at most 128 MiB of HBM per device.

v0:
```python
import math

import jax
import jax.numpy as jnp
from jax import lax
from jax.sharding import PartitionSpec as P

H = 6
HD = 64


EPS = 1e-06
GELU_C = 0.7978845608028654


def norm_rows(values):
    centred = values - jnp.mean(values, axis=-1, keepdims=True)
    recip = lax.rsqrt(jnp.mean(centred * centred, axis=-1, keepdims=True) + EPS)
    return (centred * recip, recip)


def norm_back(grad, normed, recip):
    return recip * (
        grad
        - jnp.mean(grad, axis=-1, keepdims=True)
        - normed * jnp.mean(grad * normed, axis=-1, keepdims=True)
    )


def gelu_parts(upper):
    inner = GELU_C * (upper + 0.044715 * upper * upper * upper)
    tanh_v = jnp.tanh(inner)
    value = 0.5 * upper * (1.0 + tanh_v)
    slope = 0.5 * (1.0 + tanh_v) + 0.5 * upper * (1.0 - tanh_v * tanh_v) * GELU_C * (
        1.0 + 3.0 * 0.044715 * upper * upper
    )
    return (value, slope)


def attention_scores(query, keys):
    return jnp.einsum("bqhd,bkhd->bhqk", query, keys, preferred_element_type=jnp.float32) * (
        1.0 / math.sqrt(HD)
    )


def table_lookup(indices, table):
    onehot = (indices[:, None] == jnp.arange(table.shape[0], dtype=jnp.int32)[None, :]).astype(
        jnp.float32
    )
    return jnp.dot(onehot, table, precision=lax.Precision.HIGHEST)


def layer_forward(latents, cond, weights):
    w_ada, b_ada, w_qkv, b_qv, w_out, b_out, w_up, b_up, w_down, b_down = weights
    batch, length, width = latents.shape
    rows = batch * length
    silu_b = jax.nn.silu(cond).astype(jnp.bfloat16)
    modul = jnp.dot(silu_b, w_ada, preferred_element_type=jnp.float32) + b_ada.astype(jnp.float32)
    shift1, scale1, gate1, shift2, scale2, gate2 = [
        modul[:, None, i * width : (i + 1) * width] for i in range(6)
    ]
    lat32 = latents.astype(jnp.float32)
    normed1, recip1 = norm_rows(lat32)
    attn_in = (normed1 * (1.0 + scale1) + shift1).astype(jnp.bfloat16).reshape(rows, width)
    bias_full = jnp.concatenate(
        [
            b_qv[:width].astype(jnp.float32),
            jnp.zeros((width,), jnp.float32),
            b_qv[width:].astype(jnp.float32),
        ]
    )
    proj = (jnp.dot(attn_in, w_qkv, preferred_element_type=jnp.float32) + bias_full).astype(
        jnp.bfloat16
    )
    split = proj.reshape(batch, length, 3, H, HD)
    query, keys, values = (split[:, :, 0], split[:, :, 1], split[:, :, 2])
    scores = attention_scores(query, keys)
    top = jnp.max(scores, axis=-1, keepdims=True)
    lse = top + jnp.log(jnp.sum(jnp.exp(scores - top), axis=-1, keepdims=True))
    probs = jnp.exp(scores - lse).astype(jnp.bfloat16)
    heads_out = (
        jnp.einsum("bhqk,bkhd->bqhd", probs, values, preferred_element_type=jnp.float32)
        .astype(jnp.bfloat16)
        .reshape(rows, width)
    )
    attended = (
        jnp.dot(heads_out, w_out, preferred_element_type=jnp.float32) + b_out.astype(jnp.float32)
    ).reshape(batch, length, width)
    mid = lat32 + gate1 * attended
    normed2, recip2 = norm_rows(mid)
    mlp_in = (normed2 * (1.0 + scale2) + shift2).astype(jnp.bfloat16).reshape(rows, width)
    upper = jnp.dot(mlp_in, w_up, preferred_element_type=jnp.float32) + b_up.astype(jnp.float32)
    act, slope = gelu_parts(upper)
    act_b = act.astype(jnp.bfloat16)
    down = (
        jnp.dot(act_b, w_down, preferred_element_type=jnp.float32) + b_down.astype(jnp.float32)
    ).reshape(batch, length, width)
    block_out = mid + gate2 * down
    saved = (
        cond,
        silu_b,
        modul,
        normed1,
        recip1,
        attn_in,
        query,
        keys,
        values,
        lse,
        heads_out,
        attended,
        normed2,
        recip2,
        mlp_in,
        slope,
        act_b,
        down,
    )
    return (block_out, saved)


def layer_backward(cotangent, saved, weights):
    w_ada, b_ada, w_qkv, b_qv, w_out, b_out, w_up, b_up, w_down, b_down = weights
    (
        cond,
        silu_b,
        modul,
        normed1,
        recip1,
        attn_in,
        query,
        keys,
        values,
        lse,
        heads_out,
        attended,
        normed2,
        recip2,
        mlp_in,
        slope,
        act_b,
        down,
    ) = saved
    batch, length, width = normed1.shape
    rows = batch * length
    shift1, scale1, gate1, shift2, scale2, gate2 = [
        modul[:, None, i * width : (i + 1) * width] for i in range(6)
    ]
    dout = cotangent.astype(jnp.float32)
    dgate2 = jnp.sum(dout * down, axis=1)
    dmlp = (dout * gate2).astype(jnp.bfloat16).reshape(rows, width)
    grad_w_down = jnp.dot(act_b.T, dmlp, preferred_element_type=jnp.float32)
    grad_b_down = jnp.sum(dmlp.astype(jnp.float32), axis=0)
    dupper = (jnp.dot(dmlp, w_down.T, preferred_element_type=jnp.float32) * slope).astype(
        jnp.bfloat16
    )
    grad_w_up = jnp.dot(mlp_in.T, dupper, preferred_element_type=jnp.float32)
    grad_b_up = jnp.sum(dupper.astype(jnp.float32), axis=0)
    dmlp_in = jnp.dot(dupper, w_up.T, preferred_element_type=jnp.float32).reshape(
        batch, length, width
    )
    dscale2 = jnp.sum(dmlp_in * normed2, axis=1)
    dshift2 = jnp.sum(dmlp_in, axis=1)
    dmid = dout + norm_back(dmlp_in * (1.0 + scale2), normed2, recip2)
    dgate1 = jnp.sum(dmid * attended, axis=1)
    dattn = (dmid * gate1).astype(jnp.bfloat16).reshape(rows, width)
    grad_w_out = jnp.dot(heads_out.T, dattn, preferred_element_type=jnp.float32)
    grad_b_out = jnp.sum(dattn.astype(jnp.float32), axis=0)
    dheads = (
        jnp.dot(dattn, w_out.T, preferred_element_type=jnp.float32)
        .astype(jnp.bfloat16)
        .reshape(batch, length, H, HD)
    )
    probs32 = jnp.exp(attention_scores(query, keys) - lse)
    probs_b = probs32.astype(jnp.bfloat16)
    dvalues = jnp.einsum("bhqk,bqhd->bkhd", probs_b, dheads, preferred_element_type=jnp.float32)
    dprobs = jnp.einsum("bqhd,bkhd->bhqk", dheads, values, preferred_element_type=jnp.float32)
    delta = jnp.sum(probs32 * dprobs, axis=-1, keepdims=True)
    dscores = (probs32 * (dprobs - delta)).astype(jnp.bfloat16)
    scale = 1.0 / math.sqrt(HD)
    dquery = (
        jnp.einsum("bhqk,bkhd->bqhd", dscores, keys, preferred_element_type=jnp.float32) * scale
    )
    dkeys = (
        jnp.einsum("bhqk,bqhd->bkhd", dscores, query, preferred_element_type=jnp.float32) * scale
    )
    dproj = (
        jnp.stack([dquery, dkeys, dvalues], axis=2).astype(jnp.bfloat16).reshape(rows, 3 * width)
    )
    grad_w_qkv = jnp.dot(attn_in.T, dproj, preferred_element_type=jnp.float32)
    column_sums = jnp.sum(dproj.astype(jnp.float32), axis=0)
    grad_b_qv = jnp.concatenate([column_sums[:width], column_sums[2 * width :]])
    dattn_in = jnp.dot(dproj, w_qkv.T, preferred_element_type=jnp.float32).reshape(
        batch, length, width
    )
    dscale1 = jnp.sum(dattn_in * normed1, axis=1)
    dshift1 = jnp.sum(dattn_in, axis=1)
    input_grad = dmid + norm_back(dattn_in * (1.0 + scale1), normed1, recip1)
    dmodul = jnp.concatenate([dshift1, dscale1, dgate1, dshift2, dscale2, dgate2], axis=-1)
    grad_b_ada = jnp.sum(dmodul, axis=0)
    grad_w_ada = jnp.dot(silu_b.astype(jnp.float32).T, dmodul, precision=lax.Precision.HIGHEST)
    sig = jax.nn.sigmoid(cond)
    cond_grad = jnp.dot(dmodul, w_ada.astype(jnp.float32).T, precision=lax.Precision.HIGHEST) * (
        sig * (1.0 + cond * (1.0 - sig))
    )
    grads = (
        grad_w_ada,
        grad_b_ada,
        grad_w_qkv,
        grad_b_qv,
        grad_w_out,
        grad_b_out,
        grad_w_up,
        grad_b_up,
        grad_w_down,
        grad_b_down,
    )
    return (input_grad, cond_grad, grads)


def body(
    latents,
    cotangent,
    timesteps,
    labels,
    time_table,
    class_table,
    w_ada,
    b_ada,
    w_qkv,
    b_qv,
    w_out,
    b_out,
    w_up,
    b_up,
    w_down,
    b_down,
):
    weights = (
        lax.all_gather(w_ada, "shard", axis=0, tiled=True),
        lax.all_gather(b_ada, "shard", axis=0, tiled=True),
        lax.all_gather(w_qkv, "shard", axis=0, tiled=True),
        lax.all_gather(b_qv, "shard", axis=0, tiled=True),
        lax.all_gather(w_out, "shard", axis=0, tiled=True),
        lax.all_gather(b_out, "shard", axis=0, tiled=True),
        lax.all_gather(w_up, "shard", axis=0, tiled=True),
        lax.all_gather(b_up, "shard", axis=0, tiled=True),
        lax.all_gather(w_down, "shard", axis=0, tiled=True),
        lax.all_gather(b_down, "shard", axis=0, tiled=True),
    )
    cond = table_lookup(timesteps, time_table) + table_lookup(labels, class_table)
    block_out, saved = layer_forward(latents, cond, weights)
    weights_back = (
        lax.all_gather(w_ada, "shard", axis=0, tiled=True),
        lax.all_gather(b_ada, "shard", axis=0, tiled=True),
        lax.all_gather(w_qkv, "shard", axis=0, tiled=True),
        lax.all_gather(b_qv, "shard", axis=0, tiled=True),
        lax.all_gather(w_out, "shard", axis=0, tiled=True),
        lax.all_gather(b_out, "shard", axis=0, tiled=True),
        lax.all_gather(w_up, "shard", axis=0, tiled=True),
        lax.all_gather(b_up, "shard", axis=0, tiled=True),
        lax.all_gather(w_down, "shard", axis=0, tiled=True),
        lax.all_gather(b_down, "shard", axis=0, tiled=True),
    )
    input_grad, cond_grad, grads = layer_backward(cotangent, saved, weights_back)
    owned = (
        lax.psum_scatter(grads[0], "shard", scatter_dimension=0, tiled=True),
        lax.psum_scatter(grads[1], "shard", scatter_dimension=0, tiled=True),
        lax.psum_scatter(grads[2], "shard", scatter_dimension=0, tiled=True),
        lax.psum_scatter(grads[3], "shard", scatter_dimension=0, tiled=True),
        lax.psum_scatter(grads[4], "shard", scatter_dimension=0, tiled=True),
        lax.psum_scatter(grads[5], "shard", scatter_dimension=0, tiled=True),
        lax.psum_scatter(grads[6], "shard", scatter_dimension=0, tiled=True),
        lax.psum_scatter(grads[7], "shard", scatter_dimension=0, tiled=True),
        lax.psum_scatter(grads[8], "shard", scatter_dimension=0, tiled=True),
        lax.psum_scatter(grads[9], "shard", scatter_dimension=0, tiled=True),
    )
    summed = lax.psum(
        (
            owned[0],
            owned[1],
            owned[2],
            owned[3],
            owned[4],
            owned[5],
            owned[6],
            owned[7],
            owned[8],
            owned[9],
        ),
        "rep",
    )
    return (
        block_out,
        input_grad,
        cond_grad,
        summed[0],
        summed[1],
        summed[2],
        summed[3],
        summed[4],
        summed[5],
        summed[6],
        summed[7],
        summed[8],
        summed[9],
    )


def solution(mesh):
    placed = (
        P(("shard", "rep"), None, None),
        P(("shard", "rep"), None, None),
        P(("shard", "rep")),
        P(("shard", "rep")),
        P(),
        P(),
        P("shard", None),
        P("shard"),
        P("shard", None),
        P("shard"),
        P("shard", None),
        P("shard"),
        P("shard", None),
        P("shard"),
        P("shard", None),
        P("shard"),
    )
    return jax.shard_map(
        body,
        mesh=mesh,
        in_specs=placed,
        out_specs=(
            P(("shard", "rep"), None, None),
            P(("shard", "rep"), None, None),
            P(("shard", "rep"), None),
            P("shard", None),
            P("shard"),
            P("shard", None),
            P("shard"),
            P("shard", None),
            P("shard"),
            P("shard", None),
            P("shard"),
            P("shard", None),
            P("shard"),
        ),
        check_vma=False,
    )
```

profile of v0, /device:TPU:0, one launch (start us, length us, event | category | flops | bytes accessed | tf_op | source)
XLA Modules:
  0.0 404.0 jit_solution(4812516753712237030)
XLA Ops:
  15.2 9.5 %all-gather = bf16[4,1,384]{2,1,0:T(2,128)(2,1)S(1)} all-gather(bf16[1,1,384]{2,1,0:T(2,128)(2,1)S(1)} %reshape.166), channel_id=1, replica_groups=mesh['shard'=4,'rep'=8] {'shard'}, dimensions={0}, use_global_device_ids=true | all-gather | bytes 3840 | tf_op jit(solution)/shard_map/all_gather | solution.py:247
  25.8 15.3 %all-reduce.12 = (bf16[2304]{0:T(1024)(128)(2,1)S(1)}, bf16[768]{0:T(1024)(128)(2,1)S(1)}, bf16[384]{0:T(512)(128)(2,1)S(1)}, bf16[384]{0:T(512)(128)(2,1)S(1)}) all-reduce(bf16[2304]{0:T(1024)(128)(2,1)S(1)} %dynamic-update-slice, bf16[768]{0:T(1024)(128)(2,1)S(1)} %dynamic-update-slice.1, ...), channel_id=1, replica_groups=mesh['shard'=4,'rep'=8] {'shard'}, use_global_device_ids=true, to_apply=%add | all-reduce | flops 3840 | bytes 15360
  41.1 10.6 %all_gather.39 = bf16[384,384]{1,0:T(8,128)(2,1)} all-gather(bf16[96,384]{1,0:T(8,128)(2,1)S(1)} %copy-done.34), channel_id=1, replica_groups=mesh['shard'=4,'rep'=8] {'shard'}, dimensions={0}, use_global_device_ids=true | all-gather | bytes 368640 | tf_op jit(solution)/shard_map/all_gather | solution.py:244
  51.7 12.6 %all_gather.37 = bf16[384,1152]{1,0:T(8,128)(2,1)S(1)} all-gather(bf16[96,1152]{1,0:T(8,128)(2,1)S(1)} %copy-done.32), channel_id=1, replica_groups=mesh['shard'=4,'rep'=8] {'shard'}, dimensions={0}, use_global_device_ids=true | all-gather | bytes 1105920 | tf_op jit(solution)/shard_map/all_gather | solution.py:242
  64.3 2.3 fusion.41
  69.5 2.4 fusion.7
  71.9 6.8 %reshape.183 = bf16[3,256,3,6,64]{4,3,2,1,0:T(8,128)(2,1)} reshape(bf16[768,1152]{1,0:T(8,128)(2,1)} %fusion.7) | data formatting | bytes 3538944 | tf_op jit(solution)/shard_map/reshape | solution.py:75
  78.7 4.8 %fusion.49 = (bf16[3,256,1,6,64]{4,3,2,1,0:T(8,128)(2,1)}, bf16[3,256,1,6,64]{4,3,2,1,0:T(8,128)(2,1)}, bf16[3,256,1,6,64]{4,3,2,1,0:T(8,128)(2,1)}) fusion(bf16[3,256,3,6,64]{4,3,2,1,0:T(8,128)(2,1)} %reshape.183), kind=kLoop, calls=%fused_computation.112 | loop fusion | bytes 3538944 | tf_op jit(solution)/shard_map/slice | solution.py:76
  97.0 6.6 %multiply_convert_fusion.1 = (bf16[768,1536]{1,0:T(8,128)(2,1)}, f32[768,1536]{1,0:T(8,128)}) fusion(f32[1536]{0:T(1024)S(1)} %reshape.168, bf16[768,384]{1,0:T(8,128)(2,1)S(1)} %bitcast.111, bf16[384,1536]{1,0:T(8,128)(2,1)} %all-gather.7.cloned.1.call-done), kind=kOutput, calls=%fused_computation.12 | convolution fusion | flops 917766144 | bytes 8853504 | tf_op jit(solution)/shard_map/dot_general | solution.py:92
  103.6 3.3 all-gather.9.cloned.1.call-done
  106.9 6.3 %convert_reduce_fusion = (f32[1536]{0:T(1024)S(1)}, bf16[768,1536]{1,0:T(8,128)(2,1)S(1)}) fusion(f32[768,1536]{1,0:T(8,128)} %get-tuple-element.73, f32[1536]{0:T(1024)S(1)} %reshape.168, bf16[768,384]{1,0:T(8,128)(2,1)S(1)} %bitcast.118, bf16[1536,384]{1,0:T(8,128)(2,1)} %all-gather.9.cloned.1.call-done), kind=kOutput, calls=%fused_computation.9 | convolution fusion | flops 931920384 | bytes 8859648 | tf_op jit(solution)/shard_map/dot_general | solution.py:154
  116.1 3.1 convolution_add_fusion.3
  128.8 3.8 multiply_reduce_fusion
  142.5 4.5 %fusion.56 = f32[1536,384]{1,0:T(8,128)} fusion(bf16[768,1536]{1,0:T(8,128)(2,1)} %get-tuple-element.72, bf16[768,384]{1,0:T(8,128)(2,1)S(1)} %bitcast.119), kind=kOutput, calls=%fused_computation.119 | convolution fusion | flops 905969664 | bytes 5308416 | tf_op jit(solution)/shard_map/dot_general | solution.py:152
  148.1 4.2 %fusion.55 = f32[384,1536]{1,0:T(8,128)} fusion(bf16[768,384]{1,0:T(8,128)(2,1)S(1)} %bitcast.112, bf16[768,1536]{1,0:T(8,128)(2,1)} %copy-done.7), kind=kOutput, calls=%fused_computation.118 | convolution fusion | flops 905969664 | bytes 5308416 | tf_op jit(solution)/shard_map/dot_general | solution.py:157
  157.1 3.4 fusion.46
  160.5 25.3 %reduce-scatter.8.cloned.1.call-done = f32[96,1152]{1,0:T(8,128)} async-done(((f32[384,1152]{1,0:T(8,128)}), f32[96,1152]{1,0:T(8,128)}) %reduce-scatter.8.cloned.1.call-update) | async-done | bytes 442384 | tf_op jit(solution)/shard_map/reduce_scatter | solution.py:269
  185.8 40.6 %reduce-scatter.14.cloned.1.call-done = f32[384,384]{1,0:T(8,128)} async-done(((f32[1536,384]{1,0:T(8,128)}), f32[384,384]{1,0:T(8,128)}) %reduce-scatter.14.cloned.1.call-update) | async-done | bytes 589840 | tf_op jit(solution)/shard_map/reduce_scatter | solution.py:275
  226.4 40.7 %reduce-scatter.12.cloned.1.call-done = f32[96,1536]{1,0:T(8,128)} async-done(((f32[384,1536]{1,0:T(8,128)}), f32[96,1536]{1,0:T(8,128)}) %reduce-scatter.12.cloned.1.call-update) | async-done | bytes 589840 | tf_op jit(solution)/shard_map/reduce_scatter | solution.py:273
  267.2 50.6 %reduce-scatter.6.cloned.1.call-done = f32[96,2304]{1,0:T(8,128)} async-done(((f32[384,2304]{1,0:T(8,128)}), f32[96,2304]{1,0:T(8,128)}) %reduce-scatter.6.cloned.1.call-update) | async-done | bytes 884752 | tf_op jit(solution)/shard_map/reduce_scatter | solution.py:267
  320.6 15.3 %all-reduce.11 = (f32[2304]{0:T(1024)S(1)}, f32[768]{0:T(1024)S(1)}, f32[384]{0:T(512)S(1)}, f32[1536]{0:T(1024)S(1)}, f32[384]{0:T(512)S(1)}) all-reduce(f32[2304]{0:T(1024)S(1)} %reduce_sum.205, f32[768]{0:T(1024)S(1)} %pad_maximum_fusion.1, f32[384]{0:T(512)S(1)} %get-tuple-element.53, ...), channel_id=3, replica_groups=mesh['shard'=4,'rep'=8] {'shard'}, use_global_device_ids=true, to_apply=%region_20.21.clone | all-reduce | flops 5376 | bytes 43008
  336.3 15.2 %all-reduce.9 = (f32[576]{0:T(1024)}, f32[192]{0:T(256)}, f32[96]{0:T(128)}, f32[384]{0:T(512)}, f32[96]{0:T(128)}) all-reduce(f32[576]{0:T(1024)S(1)} %dynamic-slice.5, f32[192]{0:T(256)S(1)} %dynamic-slice.7, f32[96]{0:T(128)S(1)} %dynamic-slice.9, f32[384]{0:T(512)S(1)} %dynamic-slice.11, ...), channel_id=1, replica_groups=mesh['shard'=4,'rep'=8] {'rep'}, use_global_device_ids=true, to_apply=%region_21.22 | all-reduce | flops 1344 | bytes 10752 | tf_op jit(solution)/shard_map/psum | solution.py:278
  353.6 38.3 %all-reduce.15.cloned.1.call-done = (f32[96,2304]{1,0:T(8,128)}, f32[96,1152]{1,0:T(8,128)}, f32[96,384]{1,0:T(8,128)}, f32[96,1536]{1,0:T(8,128)}, f32[384,384]{1,0:T(8,128)}) async-done(((f32[96,2304]{1,0:T(8,128)}, f32[96,1152]{1,0:T(8,128)}, f32[96,384]{1,0:T(8,128)}, f32[96,1536]{1,0:T(8,128)}, f32[384,384]{1,0:T(8,128)}), (f32[96,2304]{1,0:T(8,128)}, f32[96,1152]{1,0:T(8,128)}, f32[96,384]{1,0:T(8,128)}, ...) | async-done | bytes 2654224 | tf_op jit(solution)/shard_map/psum | solution.py:278
  391.9 2.3 copy.111
  (195 shorter events, 56.9 us)
Async XLA Ops:
  7.2 59.4 %copy-start = (f32[1001,384]{1,0:T(8,128)S(1)}, f32[1001,384]{1,0:T(8,128)}, u32[]{:S(2)}) copy-start(f32[1001,384]{1,0:T(8,128)} %param.21) | copy-start | bytes 4612612
  7.2 7.6 %copy-start.3 = (bf16[3,256,384]{2,1,0:T(8,128)(2,1)S(1)}, bf16[3,256,384]{2,1,0:T(8,128)(2,1)}, u32[]{:S(2)}) copy-start(bf16[3,256,384]{2,1,0:T(8,128)(2,1)} %param.16) | copy-start | bytes 1769476
  7.2 17.6 %copy-start.39 = (bf16[96]{0:T(256)(128)(2,1)S(1)}, bf16[96]{0:T(256)(128)(2,1)}, u32[]{:S(2)}) copy-start(bf16[96]{0:T(256)(128)(2,1)} %param.27) | copy-start | bytes 580
  7.2 17.8 %copy-start.40 = (bf16[96]{0:T(256)(128)(2,1)S(1)}, bf16[96]{0:T(256)(128)(2,1)}, u32[]{:S(2)}) copy-start(bf16[96]{0:T(256)(128)(2,1)} %param.31) | copy-start | bytes 580
  7.2 18.0 %copy-start.41 = (bf16[192]{0:T(256)(128)(2,1)S(1)}, bf16[192]{0:T(256)(128)(2,1)}, u32[]{:S(2)}) copy-start(bf16[192]{0:T(256)(128)(2,1)} %param.25) | copy-start | bytes 1156
  7.2 18.3 %copy-start.35 = (bf16[576]{0:T(1024)(128)(2,1)S(1)}, bf16[576]{0:T(1024)(128)(2,1)}, u32[]{:S(2)}) copy-start(bf16[576]{0:T(1024)(128)(2,1)} %param.23) | copy-start | bytes 3460
  7.2 33.8 %copy-start.34 = (bf16[96,384]{1,0:T(8,128)(2,1)S(1)}, bf16[96,384]{1,0:T(8,128)(2,1)}, u32[]{:S(2)}) copy-start(bf16[96,384]{1,0:T(8,128)(2,1)} %param.26) | copy-start | bytes 221188
  7.3 44.4 %copy-start.32 = (bf16[96,1152]{1,0:T(8,128)(2,1)S(1)}, bf16[96,1152]{1,0:T(8,128)(2,1)}, u32[]{:S(2)}) copy-start(bf16[96,1152]{1,0:T(8,128)(2,1)} %param.24) | copy-start | bytes 663556
  7.3 60.0 %all-gather.5.cloned.1.call-start = ((), (), s32[]{:S(2)}) async-start(), calls=%async_computation.5 | async-start | bytes 2211840 | tf_op jit(solution)/shard_map/all_gather | solution.py:240
  8.0 56.3 %copy-start.36 = (s32[3]{0:T(128)S(1)}, s32[3]{0:T(128)}, u32[]{:S(2)}) copy-start(s32[3]{0:T(128)} %param.18) | copy-start | bytes 40
  8.0 89.0 %all-gather.7.cloned.1.call-start = ((), (), s32[]{:S(2)}) async-start(), calls=%async_computation.6 | async-start | bytes 1474560 | tf_op jit(solution)/shard_map/all_gather | solution.py:246
  8.8 98.2 %all-gather.9.cloned.1.call-start = ((), (), s32[]{:S(2)}) async-start(), calls=%async_computation.7 | async-start | bytes 1474560 | tf_op jit(solution)/shard_map/all_gather | solution.py:248
  9.5 151.0 %reduce-scatter.10.cloned.1.call-start = ((), (), s32[]{:S(2)}) async-start(), calls=%async_computation.10 | async-start | bytes 737280 | tf_op jit(solution)/shard_map/reduce_scatter | solution.py:271
  14.8 51.8 %copy-start.37 = (s32[3]{0:T(128)S(1)}, s32[3]{0:T(128)}, u32[]{:S(2)}) copy-start(s32[3]{0:T(128)} %param.19) | copy-start | bytes 40
  96.7 10.3 %copy-start.27 = (bf16[3,256,384]{2,1,0:T(8,128)(2,1)}, bf16[3,256,384]{2,1,0:T(8,128)(2,1)S(1)}, u32[]{:S(2)}) copy-start(bf16[3,256,384]{2,1,0:T(8,128)(2,1)S(1)} %get-tuple-element.40) | copy-start | bytes 1769476
  97.0 6.7 %copy-start.20 = (bf16[3,256,384]{2,1,0:T(8,128)(2,1)}, bf16[3,256,384]{2,1,0:T(8,128)(2,1)S(1)}, u32[]{:S(2)}) copy-start(bf16[3,256,384]{2,1,0:T(8,128)(2,1)S(1)} %add_convert_fusion) | copy-start | bytes 1769476
  106.9 6.3 %copy-start.22 = (bf16[384,1536]{1,0:T(8,128)(2,1)S(1)}, bf16[384,1536]{1,0:T(8,128)(2,1)}, u32[]{:S(2)}) copy-start(bf16[384,1536]{1,0:T(8,128)(2,1)} %all-gather.7.cloned.1.call-done) | copy-start | bytes 3538948
  124.9 60.8 %reduce-scatter.8.cloned.1.call-start = ((), (), s32[]{:S(2)}) async-start(), calls=%async_computation.9 | async-start | bytes 2211840 | tf_op jit(solution)/shard_map/reduce_scatter | solution.py:269
  126.9 5.7 %slice-start = ((s8[4718592]{0:T(1024)(128)(4,1)}), s8[524288]{0:T(1024)(128)(4,1)S(1)}, s32[]{:S(2)}) async-start(s8[4718592]{0:T(1024)(128)(4,1)} %bitcast.99), calls=%async_computation.14 | async-start | bytes 1048576
  141.5 85.0 %reduce-scatter.14.cloned.1.call-start = ((), (), s32[]{:S(2)}) async-start(), calls=%async_computation.12 | async-start | bytes 2949120 | tf_op jit(solution)/shard_map/reduce_scatter | solution.py:275
  147.1 120.1 %reduce-scatter.12.cloned.1.call-start = ((), (), s32[]{:S(2)}) async-start(), calls=%async_computation.11 | async-start | bytes 2949120 | tf_op jit(solution)/shard_map/reduce_scatter | solution.py:273
  152.3 165.4 %reduce-scatter.6.cloned.1.call-start = ((), (), s32[]{:S(2)}) async-start(), calls=%async_computation.8 | async-start | bytes 4423680 | tf_op jit(solution)/shard_map/reduce_scatter | solution.py:267
  160.5 191.0 %copy-start.8 = (bf16[384,2304]{1,0:T(8,128)(2,1)S(1)}, bf16[384,2304]{1,0:T(8,128)(2,1)}, u32[]{:S(2)}) copy-start(bf16[384,2304]{1,0:T(8,128)(2,1)} %all-gather.5.cloned.1.call-done) | copy-start | bytes 5308420
  160.5 231.4 %all-reduce.15.cloned.1.call-start = ((), (), s32[]{:S(2)}) async-start(), calls=%async_computation.13 | async-start | bytes 5308416 | tf_op jit(solution)/shard_map/psum | solution.py:278
  (29 other events, 69.0 us)
Sparse Core Ops, SparseCore 0:
  9.9 36.7 all-gather.4
  48.5 28.7 all-gather.6
  79.2 27.7 all-gather.8
  125.1 25.0 reduce-scatter.9
  153.3 32.4 reduce-scatter.7
  189.0 37.3 reduce-scatter.13
  229.8 37.3 reduce-scatter.11
  270.5 47.1 reduce-scatter.5
  320.8 71.0 all-reduce.14
where the time goes:
time: 409 us; the launch traced here: 404 us
  waiting for transfers between devices  201 us (49%)
  blocking collectives  78.5 us (19%)
  matrix products  54.1 us (13%)
  local copies, waits for them, and re-layouts  40.6 us (10%)
  between operations  19.3 us (5%)
  other arithmetic  9.81 us (2%)
    reduce_scatter x1, waiting for transfers between devices, body(): lax.psum_scatter(grads[0], 'shard', scatter_dimension=0, tiled=True)  50.6 us
    reduce_scatter x1, waiting for transfers between devices, body(): lax.psum_scatter(grads[6], 'shard', scatter_dimension=0, tiled=True)  40.7 us
    reduce_scatter x1, waiting for transfers between devices, body(): lax.psum_scatter(grads[8], 'shard', scatter_dimension=0, tiled=True)  40.6 us
    psum x1, waiting for transfers between devices, body(): lax.psum((owned[0], owned[1], owned[2], owned[3], owned[4], owned[5], own...  38.3 us
    unnamed x2, blocking collectives  30.6 us
    reduce_scatter x1, waiting for transfers between devices, body(): lax.psum_scatter(grads[2], 'shard', scatter_dimension=0, tiled=True)  25.3 us
    unnamed x118, local copies, waits for them, and re-layouts  23 us
    psum x1, blocking collectives, body(): lax.psum((owned[0], owned[1], owned[2], owned[3], owned[4], owned[5], own...  15.2 us
  transfers between devices with their start and end apart: 9, of which 6 were waited for; matrix products, arithmetic and copies ran while one was open for 19% of the time, Pallas kernels for 0%

commit v1 on v0

v1 whole, which is shorter than its diff:
```python
import functools
import math

import jax
import jax.numpy as jnp
from jax import lax
from jax.experimental import pallas as pl
from jax.experimental.pallas import tpu as pltpu
from jax.sharding import PartitionSpec as P

H = 6
HD = 64
D = 384
TILES = 12
EPS = 1e-06
GELU_C = 0.7978845608028654
MESH = pl.DeviceIdType.MESH
F32 = jnp.float32
BF16 = jnp.bfloat16
MIB = 1024 * 1024


def mm(a, b):
    return lax.dot_general(a, b, (((1,), (0,)), ((), ())), preferred_element_type=F32)


def mm_bt(a, b):
    return lax.dot_general(a, b, (((1,), (1,)), ((), ())), preferred_element_type=F32)


def mm_at(a, b):
    return lax.dot_general(a, b, (((0,), (0,)), ((), ())), preferred_element_type=F32)


def row(vals):
    return jnp.mean(vals, axis=-1, keepdims=True)


def cols(vals):
    return jnp.sum(vals, axis=0, keepdims=True)


def barrier(peers):
    sem = pltpu.get_barrier_semaphore()
    for peer in peers:
        pl.semaphore_signal(sem, inc=1, device_id=peer, device_id_type=MESH)
    pl.semaphore_wait(sem, len(peers))


def remote(src, dst, send, recv, peer):
    return pltpu.make_async_remote_copy(
        src_ref=src, dst_ref=dst, send_sem=send, recv_sem=recv, device_id=peer, device_id_type=MESH
    )


def gather_kernel(
    n, w0, w1, w2, w3, wada, silu, bada, bias,
    o0, o1, o2, o3, omod, obias,
    silu_buf, mod_send, mod_buf, bias_buf,
    g_send, g_recv, f_send, f_recv, s_send, s_recv, m_send, m_recv, b_send, b_recv,
):
    me = lax.axis_index("shard")
    rep = lax.axis_index("rep")
    core = lax.rem(rep, 2)
    sibling = (me, rep + 1 - 2 * core)
    peers = [(lax.rem(me + d, n), rep) for d in range(1, n)]
    barrier(peers + [sibling])

    small = []
    for d in range(1, n):
        peer = peers[d - 1]
        cp = remote(silu.at[peer[0]], silu_buf.at[me], s_send.at[d], s_recv.at[d], peer)
        cp.start()
        bp = remote(bias, bias_buf.at[me], b_send.at[d], b_recv.at[d], peer)
        bp.start()
        small.append((cp, bp))

    mats = [(w0, o0), (w1, o1), (w2, o2), (w3, o3)]
    pushes = {}
    for m, (w, o) in enumerate(mats):
        rows = w.shape[0]
        half = rows // 2
        mine = pl.multiple_of(core * half, 16)
        for d in (1, 3, 2) if n == 4 else range(1, n):
            cp = remote(
                w.at[pl.ds(mine, half)],
                o.at[pl.ds(pl.multiple_of(me * rows + core * half, 16), half)],
                g_send.at[m, d], g_recv.at[m, d], peers[d - 1],
            )
            cp.start()
            pushes[m, d] = cp
    for w, o in mats:
        rows = w.shape[0]
        o[pl.ds(pl.multiple_of(me * rows, 16), rows), :] = w[...]

    silu_buf[me] = silu[me]
    for cp, _ in small:
        cp.wait_recv()
    part = mm(silu_buf[...].reshape(n * 16, silu.shape[2]), wada[...])
    bada_v = bada[...]
    for p in range(n):
        mod_send[p] = part[p * 16 : p * 16 + 8] + bada_v
    mods = []
    for d in range(1, n):
        peer = peers[d - 1]
        cp = remote(mod_send.at[peer[0]], mod_buf.at[me], m_send.at[d], m_recv.at[d], peer)
        cp.start()
        mods.append(cp)
    mod_buf[me] = mod_send[me]
    bias_buf[me] = bias[...]
    for _, bp in small:
        bp.wait_recv()
    total = bias_buf[0]
    for p in range(1, n):
        total = total + bias_buf[p]
    obias[...] = total
    for cp in mods:
        cp.wait_recv()
    total = mod_buf[0]
    for p in range(1, n):
        total = total + mod_buf[p]
    omod[...] = total

    passed = []
    for m, (w, o) in enumerate(mats):
        rows = w.shape[0]
        half = rows // 2
        for d in (1, 3, 2) if n == 4 else range(1, n):
            pushes[m, d].wait_recv()
            origin = lax.rem(me - d + n, n)
            spot = pl.ds(pl.multiple_of(origin * rows + core * half, 16), half)
            cp = remote(o.at[spot], o.at[spot], f_send.at[m, d], f_recv.at[m, d], sibling)
            cp.start()
            passed.append(cp)
    for cp in passed:
        cp.wait()
    for cp in pushes.values():
        cp.wait_send()
    for cp, bp in small:
        cp.wait_send()
        bp.wait_send()
    for cp in mods:
        cp.wait_send()


def gather_weights(n, w_qkv, w_out, w_up, w_down, w_ada, silu, bada, bias):
    mats = (w_qkv, w_out, w_up, w_down)
    vmem = pl.BlockSpec(memory_space=pltpu.VMEM)
    dma = pltpu.SemaphoreType.DMA
    return pl.pallas_call(
        functools.partial(gather_kernel, n),
        out_shape=[jax.ShapeDtypeStruct((n * w.shape[0], w.shape[1]), BF16) for w in mats]
        + [jax.ShapeDtypeStruct(bada.shape[:0] + (8, bada.shape[1]), F32), jax.ShapeDtypeStruct(bias.shape, F32)],
        in_specs=[vmem] * 8,
        out_specs=[vmem] * 6,
        scratch_shapes=[
            pltpu.VMEM(silu.shape, BF16),
            pltpu.VMEM((n, 8, bada.shape[1]), F32),
            pltpu.VMEM((n, 8, bada.shape[1]), F32),
            pltpu.VMEM((n,) + bias.shape, F32),
            dma((4, n)), dma((4, n)), dma((4, n)), dma((4, n)),
            dma((n,)), dma((n,)), dma((n,)), dma((n,)), dma((n,)), dma((n,)),
        ],
        compiler_params=pltpu.CompilerParams(
            collective_id=0, has_side_effects=True, vmem_limit_bytes=32 * MIB
        ),
        name="gather_weights",
    )(*mats, w_ada, silu, bada, bias)


def block_kernel(
    lat_ref, cot_ref, mod_ref, bias_ref, wqkv, wout, wup, wdown,
    out_ref, ing_ref, dmod_ref, pg_ref, gb_ref,
    acc, proj_s, prob_s, heads_s, act_s, slope_s, dproj_s,
):
    step = pl.program_id(0)
    last = pl.num_programs(0) - 1

    @pl.when(step == 0)
    def _():
        acc[...] = jnp.zeros_like(acc)
        gb_ref[...] = jnp.zeros_like(gb_ref)

    mod = mod_ref[0]
    shift1, scale1, gate1, shift2, scale2, gate2 = [mod[i : i + 1] for i in range(6)]
    bias = bias_ref[...]
    lat = lat_ref[0].astype(F32)
    centred = lat - row(lat)
    recip1 = lax.rsqrt(row(centred * centred) + EPS)
    normed1 = centred * recip1
    attn_in = (normed1 * (1.0 + scale1) + shift1).astype(BF16)
    for j in range(3):
        part = mm(attn_in, wqkv[:, j * D : (j + 1) * D])
        if j == 0:
            part = part + bias[0:1]
        if j == 2:
            part = part + bias[1:2]
        proj_s[:, j * D : (j + 1) * D] = part.astype(BF16)

    low = lax.broadcasted_iota(jnp.int32, (256, 128), 1) < HD
    zero = jnp.zeros((256, 128), BF16)
    scale = 1.0 / math.sqrt(HD)
    for pair in range(H // 2):
        at = pair * 128
        q = proj_s[:, at : at + 128]
        k = proj_s[:, D + at : D + at + 128]
        v = proj_s[:, 2 * D + at : 2 * D + at + 128]
        outs = []
        for side in range(2):
            qm = jnp.where(low, q, zero) if side == 0 else jnp.where(low, zero, q)
            s = mm_bt(qm, k) * scale
            e = jnp.exp(s - jnp.max(s, axis=-1, keepdims=True))
            p = e * (1.0 / jnp.sum(e, axis=-1, keepdims=True))
            prob_s[2 * pair + side] = p
            outs.append(mm(p.astype(BF16), v))
        heads_s[:, at : at + 128] = jnp.where(low, outs[0], outs[1]).astype(BF16)

    attended = mm(heads_s[...], wout[...]) + bias[2:3]
    mid = lat + gate1 * attended
    centred = mid - row(mid)
    recip2 = lax.rsqrt(row(centred * centred) + EPS)
    normed2 = centred * recip2
    mlp_in = (normed2 * (1.0 + scale2) + shift2).astype(BF16)
    down = jnp.zeros((256, D), F32)
    for j in range(4):
        at = slice(j * D, (j + 1) * D)
        u = mm(mlp_in, wup[:, at]) + bias[3 + j : 4 + j]
        sq = u * u
        t = jnp.tanh(GELU_C * u * (1.0 + 0.044715 * sq))
        half = 0.5 * (1.0 + t)
        act = (u * half).astype(BF16)
        act_s[:, at] = act
        slope_s[:, at] = half + 0.5 * u * (1.0 - t * t) * (GELU_C + 3.0 * 0.044715 * GELU_C * sq)
        down = down + mm(act, wdown[at, :])
    down = down + bias[7:8]
    out_ref[0] = mid + gate2 * down

    dout = cot_ref[0].astype(F32)
    dmod_ref[0, 5:6, :] = cols(dout * down)
    dmlp = (dout * gate2).astype(BF16)
    gb_ref[7:8, :] += cols(dmlp.astype(F32))
    dmlp_in = jnp.zeros((256, D), F32)
    for j in range(4):
        at = slice(j * D, (j + 1) * D)
        acc[8 + j] += mm_at(act_s[:, at], dmlp)
        dup = (mm_bt(dmlp, wdown[at, :]) * slope_s[:, at]).astype(BF16)
        gb_ref[3 + j : 4 + j, :] += cols(dup.astype(F32))
        acc[4 + j] += mm_at(mlp_in, dup)
        dmlp_in = dmlp_in + mm_bt(dup, wup[:, at])
    dmod_ref[0, 4:5, :] = cols(dmlp_in * normed2)
    dmod_ref[0, 3:4, :] = cols(dmlp_in)
    g2 = dmlp_in * (1.0 + scale2)
    dmid = dout + recip2 * (g2 - row(g2) - normed2 * row(g2 * normed2))
    dmod_ref[0, 2:3, :] = cols(dmid * attended)
    dattn = (dmid * gate1).astype(BF16)
    gb_ref[2:3, :] += cols(dattn.astype(F32))
    acc[3] += mm_at(heads_s[...], dattn)
    dheads = mm_bt(dattn, wout[...]).astype(BF16)
    for pair in range(H // 2):
        at = pair * 128
        q = proj_s[:, at : at + 128]
        k = proj_s[:, D + at : D + at + 128]
        v = proj_s[:, 2 * D + at : 2 * D + at + 128]
        dh = dheads[:, at : at + 128]
        dqs, dks, dvs = [], [], []
        for side in range(2):
            p = prob_s[2 * pair + side]
            dhm = jnp.where(low, dh, zero) if side == 0 else jnp.where(low, zero, dh)
            dvs.append(mm_at(p.astype(BF16), dh))
            dp = mm_bt(dhm, v)
            delta = jnp.sum(p * dp, axis=-1, keepdims=True)
            ds = (p * (dp - delta)).astype(BF16)
            dqs.append(mm(ds, k))
            dks.append(mm_at(ds, q))
        dproj_s[:, at : at + 128] = (jnp.where(low, dqs[0], dqs[1]) * scale).astype(BF16)
        dproj_s[:, D + at : D + at + 128] = (jnp.where(low, dks[0], dks[1]) * scale).astype(BF16)
        dproj_s[:, 2 * D + at : 2 * D + at + 128] = jnp.where(low, dvs[0], dvs[1]).astype(BF16)
    dattn_in = jnp.zeros((256, D), F32)
    for j in range(3):
        at = slice(j * D, (j + 1) * D)
        dpj = dproj_s[:, at]
        acc[j] += mm_at(attn_in, dpj)
        dattn_in = dattn_in + mm_bt(dpj, wqkv[:, at])
        if j != 1:
            gb_ref[j // 2 : j // 2 + 1, :] += cols(dpj.astype(F32))
    dmod_ref[0, 1:2, :] = cols(dattn_in * normed1)
    dmod_ref[0, 0:1, :] = cols(dattn_in)
    g1 = dattn_in * (1.0 + scale1)
    ing_ref[0] = dmid + recip1 * (g1 - row(g1) - normed1 * row(g1 * normed1))

    @pl.when(step == last)
    def _():
        for s in range(4):
            for t in range(8):
                pg_ref[s, t * 96 : (t + 1) * 96, :] = acc[t, s * 96 : (s + 1) * 96, :].astype(BF16)
            pg_ref[s, 768:1152, :] = acc[8 + s].astype(BF16)


def run_block(latents, cotangent, modul, bias, wqkv, wout, wup, wdown):
    batch, length, width = latents.shape
    tok = pl.BlockSpec((1, length, width), lambda i: (i, 0, 0))
    mod = pl.BlockSpec((1, 6, width), lambda i: (i, 0, 0))
    whole = pl.BlockSpec(memory_space=pltpu.VMEM)
    return pl.pallas_call(
        block_kernel,
        grid=(batch,),
        in_specs=[tok, tok, mod] + [whole] * 5,
        out_specs=[tok, tok, mod, whole, whole],
        out_shape=[
            jax.ShapeDtypeStruct(latents.shape, F32),
            jax.ShapeDtypeStruct(latents.shape, F32),
            jax.ShapeDtypeStruct((batch, 6, width), F32),
            jax.ShapeDtypeStruct((4, 96 * TILES, width), BF16),
            jax.ShapeDtypeStruct((8, width), F32),
        ],
        scratch_shapes=[
            pltpu.VMEM((TILES, D, D), F32),
            pltpu.VMEM((length, 3 * D), BF16),
            pltpu.VMEM((H, length, length), F32),
            pltpu.VMEM((length, D), BF16),
            pltpu.VMEM((length, 4 * D), BF16),
            pltpu.VMEM((length, 4 * D), F32),
            pltpu.VMEM((length, 3 * D), BF16),
        ],
        compiler_params=pltpu.CompilerParams(
            dimension_semantics=("arbitrary",), vmem_limit_bytes=48 * MIB
        ),
        cost_estimate=pl.CostEstimate(flops=9 * 10**9, bytes_accessed=12 * 10**6, transcendentals=2 * 10**6),
        name="block",
    )(latents, cotangent, modul, bias, wqkv, wout, wup, wdown)


def reduce_kernel(
    n, nz, pg, pay, out, pays,
    sib_buf, chip, grp_buf, mine, z_buf,
    a_send, a_recv, b_send, b_recv, c_send, c_recv, d_send, d_recv, e_send, e_recv,
    pz_send, pz_recv, ps_send, ps_recv, pc_send, pc_recv,
):
    me = lax.axis_index("shard")
    rep = lax.axis_index("rep")
    core = lax.rem(rep, 2)
    z = rep // 2
    sibling = (me, rep + 1 - 2 * core)
    speers = [(lax.rem(me + d, n), rep) for d in range(1, n)]
    zs = [lax.rem(z + d, nz) for d in range(nz)]
    zpeers = [(me, zs[d] * 2 + core) for d in range(1, nz)]
    barrier([sibling] + speers + zpeers)
    half = pg.shape[1] // 2
    chunk = half // nz
    own = pl.ds(pl.multiple_of(core * half, 16), half)
    other = pl.ds(pl.multiple_of((1 - core) * half, 16), half)

    order = [1, 3, 2, 0] if n == 4 else list(range(1, n)) + [0]
    firsts = {}
    for d in order:
        s = lax.rem(me + d, n)
        cp = remote(pg.at[s, other], sib_buf.at[s], a_send.at[d], a_recv.at[d], sibling)
        cp.start()
        firsts[d] = cp
    pz = []
    for d in range(1, nz):
        cp = remote(pay, pays.at[core, me, z], pz_send.at[d], pz_recv.at[d], zpeers[d - 1])
        cp.start()
        pz.append(cp)
    pays[core, me, z] = pay[...]
    seconds = {}
    for d in order:
        s = lax.rem(me + d, n)
        firsts[d].wait_recv()
        both = pg[s, own, :].astype(F32) + sib_buf[s].astype(F32)
        chip[s] = both.astype(BF16)
        if d:
            cp = remote(chip.at[s], grp_buf.at[me], b_send.at[d], b_recv.at[d], speers[d - 1])
            cp.start()
            seconds[d] = cp
    for cp in pz:
        cp.wait_recv()
    ps = []
    for d in range(1, n):
        cp = remote(pays.at[core, me], pays.at[core, me], ps_send.at[d], ps_recv.at[d], speers[d - 1])
        cp.start()
        ps.append(cp)
    for d in range(1, n):
        seconds[d].wait_recv()
    total = chip[me].astype(F32)
    for d in range(1, n):
        total = total + grp_buf[lax.rem(me + d, n)].astype(F32)
    mine[...] = total.astype(BF16)
    thirds = []
    for d in range(1, nz):
        spot = pl.ds(pl.multiple_of(zs[d] * chunk, 16), chunk)
        cp = remote(mine.at[spot], z_buf.at[z], c_send.at[d], c_recv.at[d], zpeers[d - 1])
        cp.start()
        thirds.append(cp)
    for cp in ps:
        cp.wait_recv()
    pc = remote(pays.at[core], pays.at[core], pc_send, pc_recv, sibling)
    pc.start()
    for cp in thirds:
        cp.wait_recv()
    total = mine[pl.ds(pl.multiple_of(z * chunk, 16), chunk), :].astype(F32)
    for d in range(1, nz):
        total = total + z_buf[zs[d]].astype(F32)
    spot = pl.ds(pl.multiple_of(core * half + z * chunk, 16), chunk)
    out[spot, :] = total.astype(BF16)
    fourths = []
    for d in range(1, nz):
        cp = remote(out.at[spot], out.at[spot], d_send.at[d], d_recv.at[d], zpeers[d - 1])
        cp.start()
        fourths.append(cp)
    fifths = [remote(out.at[spot], out.at[spot], e_send.at[0], e_recv.at[0], sibling)]
    fifths[0].start()
    for d in range(1, nz):
        fourths[d - 1].wait_recv()
        origin = lax.rem(z - d + nz, nz)
        spot = pl.ds(pl.multiple_of(core * half + origin * chunk, 16), chunk)
        cp = remote(out.at[spot], out.at[spot], e_send.at[d], e_recv.at[d], sibling)
        cp.start()
        fifths.append(cp)
    for cp in fifths:
        cp.wait()
    pc.wait()
    for cp in list(firsts.values()) + list(seconds.values()) + thirds + fourths + pz + ps:
        cp.wait_send()


def reduce_grads(n, nz, pg, pay):
    vmem = pl.BlockSpec(memory_space=pltpu.VMEM)
    dma = pltpu.SemaphoreType.DMA
    rows, width = pg.shape[1:]
    half = rows // 2
    return pl.pallas_call(
        functools.partial(reduce_kernel, n, nz),
        out_shape=[
            jax.ShapeDtypeStruct((rows, width), BF16),
            jax.ShapeDtypeStruct((2, n, nz) + pay.shape, BF16),
        ],
        in_specs=[vmem] * 2,
        out_specs=[vmem] * 2,
        scratch_shapes=[
            pltpu.VMEM((n, half, width), BF16),
            pltpu.VMEM((n, half, width), BF16),
            pltpu.VMEM((n, half, width), BF16),
            pltpu.VMEM((half, width), BF16),
            pltpu.VMEM((nz, half // nz, width), BF16),
            dma((n,)), dma((n,)), dma((n,)), dma((n,)),
            dma((nz,)), dma((nz,)), dma((nz,)), dma((nz,)), dma((nz,)), dma((nz,)),
            dma((nz,)), dma((nz,)), dma((n,)), dma((n,)), dma, dma,
        ],
        compiler_params=pltpu.CompilerParams(
            collective_id=1, has_side_effects=True, vmem_limit_bytes=40 * MIB
        ),
        name="reduce_grads",
    )(pg, pay)


def place(piece, n, me):
    full = jnp.zeros((n * piece.shape[0],), F32)
    return lax.dynamic_update_slice(full, piece.astype(F32), (me * piece.shape[0],))


def body(
    n, reps,
    latents, cotangent, timesteps, labels, time_table, class_table,
    w_ada, b_ada, w_qkv, b_qv, w_out, b_out, w_up, b_up, w_down, b_down,
):
    me = lax.axis_index("shard")
    batch, length, width = latents.shape
    cond = jnp.concatenate(
        [
            lax.dynamic_slice(time_table, (timesteps[i], 0), (1, width))
            + lax.dynamic_slice(class_table, (labels[i], 0), (1, width))
            for i in range(batch)
        ]
    )
    sig = jax.nn.sigmoid(cond)
    silu_b = (cond * sig).astype(BF16)
    share = width // n
    silu = jnp.pad(
        silu_b.reshape(batch, n, share).transpose(1, 0, 2), ((0, 0), (0, 16 - batch), (0, 0))
    )
    bias = jnp.concatenate(
        [place(b_qv, n, me), place(b_out, n, me), place(b_up, n, me), place(b_down, n, me)]
    ).reshape(8, width)
    wqkv, wout, wup, wdown, modul, bias = gather_weights(
        n, w_qkv, w_out, w_up, w_down, w_ada, silu, place(b_ada, n, me)[None, :], bias
    )
    w_late, _ = lax.optimization_barrier((w_ada, modul))
    w_ada_full = lax.all_gather(w_late, "shard", axis=0, tiled=True)
    block_out, input_grad, dmod, pg, gb = run_block(
        latents, cotangent, modul[:batch].reshape(batch, 6, width), bias, wqkv, wout, wup, wdown
    )
    cond_grad = jnp.dot(
        dmod.reshape(batch, 6 * width), w_ada_full.astype(F32).T, precision=lax.Precision.HIGHEST
    ) * (sig * (1.0 + cond * (1.0 - sig)))

    used = batch * 7 + 8
    pay = jnp.concatenate(
        [
            dmod.reshape(batch * 6, width),
            silu_b.astype(F32),
            gb,
            jnp.zeros((-used % 16, width), F32),
        ]
    ).astype(BF16)
    nz = reps // 2
    if reps % 2 == 0 and pg.shape[1] % (32 * nz) == 0:
        own, pays = reduce_grads(n, nz, pg, pay)
        own = own.astype(F32)
    else:
        own = lax.psum(lax.psum_scatter(pg.astype(F32), "shard", scatter_dimension=0), "rep")
        pays = lax.all_gather(pay, ("shard", "rep"))
    pays = pays.reshape((-1,) + pay.shape)
    count = pays.shape[0] * batch
    dm = pays[:, : batch * 6].reshape(count, 6 * width)
    silu_all = pays[:, batch * 6 : batch * 7].reshape(count, width)
    silu_own = lax.dynamic_slice(silu_all, (0, me * share), (count, share))
    grad_w_ada = mm_at(silu_own, dm)
    grad_b_ada = jnp.sum(dm.astype(F32), axis=0)
    gbs = jnp.sum(pays[:, batch * 7 : used].astype(F32), axis=0).reshape(-1)

    def take(vec):
        size = vec.shape[0] // n
        return lax.dynamic_slice(vec, (me * size,), (size,))

    tiles = [own[t * 96 : (t + 1) * 96] for t in range(8)]
    return (
        block_out,
        input_grad,
        cond_grad,
        grad_w_ada,
        take(grad_b_ada),
        jnp.concatenate(tiles[0:3], axis=1),
        take(gbs[: 2 * width]),
        tiles[3],
        take(gbs[2 * width : 3 * width]),
        jnp.concatenate(tiles[4:8], axis=1),
        take(gbs[3 * width : 7 * width]),
        own[768:],
        take(gbs[7 * width :]),
    )


def solution(mesh):
    both = ("shard", "rep")
    placed = (P(both, None, None), P(both, None, None), P(both), P(both), P(), P()) + (
        P("shard", None),
        P("shard"),
    ) * 5
    return jax.shard_map(
        functools.partial(body, mesh.shape["shard"], mesh.shape["rep"]),
        mesh=mesh,
        in_specs=placed,
        out_specs=(P(both, None, None), P(both, None, None), P(both, None))
        + (P("shard", None), P("shard")) * 5,
        check_vma=False,
    )
```

time: 409 us -> 171 us (0.42)
  waiting for transfers between devices: 201 us -> 0.02 us
  Pallas kernels: 0 us -> 112 us
  blocking collectives: 78.5 us -> 0 us
  matrix products: 54.1 us -> 4.86 us
  local copies, waits for them, and re-layouts: 40.6 us -> 20.3 us
  between operations: 19.3 us -> 25.9 us
    reduce_scatter x5 -> x0, waiting for transfers between devices: 157 us -> none  [the longest x1 50.6 us: body(): lax.psum_scatter(grads[0], 'shard', scatter_dimension=0, tiled=True)]
    pallas_call x0 -> x3, Pallas kernels: none -> 112 us  [the longest x1 47.7 us: reduce_grads(): pl.pallas_call(functools.partial(reduce_kernel, n, nz), out_shape=[jax.Sh...]
    dot_general x23 -> x2, matrix products: 54.1 us -> 4.86 us  [the longest x1 3.57 us: body(): jnp.dot(dmod.reshape(batch, 6 * width), w_ada_full.astype(F32).T, precisi...]
    psum x1 -> x0, waiting for transfers between devices: 38.3 us -> none  [body(): lax.psum((owned[0], owned[1], owned[2], owned[3], owned[4], owned[5], own...]
    all_gather x3 -> x0, blocking collectives: 32.7 us -> none  [the longest x1 12.6 us: body(): lax.all_gather(w_qkv, 'shard', axis=0, tiled=True)]
    unnamed x2 -> x0, blocking collectives: 30.6 us -> none
    psum x1 -> x0, blocking collectives: 15.2 us -> none  [body(): lax.psum((owned[0], owned[1], owned[2], owned[3], owned[4], owned[5], own...]
    unnamed x118 -> x25, local copies, waits for them, and re-layouts: 23 us -> 11.6 us
  transfers between devices with their start and end apart: 9 -> 1, of which waited for: 6 -> 0; matrix products, arithmetic and copies ran while one was open for 19% -> 5% of each run, Pallas kernels for 0% -> 48%
where the time goes in v1:
time: 171 us; the launch traced here: 169 us
  Pallas kernels  112 us (65%)
  between operations  25.9 us (15%)
  local copies, waits for them, and re-layouts  20.3 us (12%)
  other arithmetic  5.78 us (3%)
  matrix products  4.86 us (3%)
    pallas_call x1, Pallas kernels, reduce_grads(): pl.pallas_call(functools.partial(reduce_kernel, n, nz), out_shape=[jax.Sh...  47.7 us
    pallas_call x1, Pallas kernels, run_block(): pl.pallas_call(block_kernel, grid=(batch,), in_specs=[tok, tok, mod] + [w...  32.5 us
    pallas_call x1, Pallas kernels, gather_weights(): pl.pallas_call(functools.partial(gather_kernel, n), out_shape=[jax.ShapeD...  31.3 us
    unnamed x25, local copies, waits for them, and re-layouts  11.6 us
    dot_general x1, matrix products, body(): jnp.dot(dmod.reshape(batch, 6 * width), w_ada_full.astype(F32).T, precisi...  3.57 us
  transfers between devices with their start and end apart: 1, of which 0 were waited for; matrix products, arithmetic and copies ran while one was open for 5% of the time, Pallas kernels for 48%

profile of v1, /device:TPU:0, one launch (start us, length us, event | category | flops | bytes accessed | tf_op | source)
XLA Modules:
  0.0 168.6 jit_solution(5494838143184966969)
XLA Ops:
  7.2 1.4 fusion.18
  11.2 1.4 fusion.19
  21.6 0.8 fusion.10
  24.2 0.8 convert_dynamic-update-slice_fusion
  24.9 0.7 convert_dynamic-update-slice_fusion.1
  26.6 1.0 copy-done.1
  27.6 1.0 copy-done.2
  28.6 1.0 copy-done.3
  29.6 0.9 copy-done.4
  30.5 0.9 copy-done.5
  31.4 31.3 %gather_weights.1 = (bf16[384,1152]{1,0:T(8,128)(2,1)S(1)}, bf16[384,384]{1,0:T(8,128)(2,1)S(1)}, bf16[384,1536]{1,0:T(8,128)(2,1)S(1)}, bf16[1536,384]{1,0:T(8,...) custom-call(bf16[96,1152]{1,0:T(8,128)(2,1)S(1)} %copy-done.4, bf16[96,384]{1,0:T(8,128)(2,1)S(1)} %copy-done.5, ...), custom_call_target="tpu_custom_call" | custom-call | tf_op jit(solution)/shard_map/gather_weights/pallas_call | solution.py:150
  62.8 0.9 copy-done.6
  64.5 1.2 copy-done.7
  65.6 1.1 copy-done.9
  66.7 1.0 copy-done.11
  67.6 32.5 %block.1 = (f32[3,256,384]{2,1,0:T(8,128)}, f32[3,256,384]{2,1,0:T(8,128)}, f32[3,6,384]{2,1,0:T(8,128)S(1)}, bf16[4,1152,384]{2,1,0:T(8,128)(2,1)}, f32[8,384]{1,0:T(8,128)S(1)}) custom-call(bf16[3,256,384]{2,1,0:T(8,128)(2,1)S(1)} %copy-done.8, bf16[3,256,384]{2,1,0:T(8,128)(2,1)S(1)} %copy-done.9, f32[3,6,384]{2,1,0:T(8,128)S(1)} %reshape.63.mod_ref, ...), custom_call_target="tpu_custom_call" | custom-call | flops 8999999488 | bytes 12000000 | tf_op jit(solution)/shard_map/block/pallas_call | solution.py:304
  100.4 2.0 %copy-done = bf16[4,1152,384]{2,1,0:T(8,128)(2,1)S(1)} copy-done((bf16[4,1152,384]{2,1,0:T(8,128)(2,1)S(1)}, bf16[4,1152,384]{2,1,0:T(8,128)(2,1)}, u32[]{:S(2)}) %copy-start) | copy-done | bytes 3538968
  102.4 47.7 %reduce_grads.1 = (bf16[1152,384]{1,0:T(8,128)(2,1)S(1)}, bf16[2,4,4,32,384]{4,3,2,1,0:T(8,128)(2,1)S(1)}) custom-call(bf16[4,1152,384]{2,1,0:T(8,128)(2,1)S(1)} %copy-done, bf16[32,384]{1,0:T(8,128)(2,1)S(1)} %maximum_maximum_fusion.pay), custom_call_target="tpu_custom_call" | custom-call | tf_op jit(solution)/shard_map/reduce_grads/pallas_call | solution.py:432
  151.7 0.9 slice.116
  154.4 0.7 fusion.16
  155.2 0.8 pad_maximum_fusion.1
  156.0 0.9 pad_maximum_fusion
  156.8 1.3 fusion
  158.1 3.6 %convolution_multiply_fusion = f32[3,384]{1,0:T(4,128)} fusion(f32[3,2304]{1,0:T(4,128)S(1)} %bitcast.25, bf16[384,2304]{1,0:T(8,128)(2,1)} %all-gather.2.cloned.1.call-done, f32[1,384]{1,0:T(1,128)S(1)} %get-tuple-element.48, f32[1,384]{1,0:T(1,128)S(1)} %get-tuple-element.50, f32[1,384]{1,0:T(1,128)S(1)} %get-tuple-element.42), kind=kOutput, calls=%fused_computation | convolution fusion | flops 31862016 | bytes 1806336 | tf_op jit(solution)/shard_map/dot_general | solution.py:493
  (58 shorter events, 7.0 us)
Async XLA Ops:
  7.2 151.0 %all-gather.2.cloned.1.call-start = ((), (), s32[]{:S(2)}) async-start(), calls=%async_computation | async-start | bytes 2211840 | tf_op jit(solution)/shard_map/all_gather | solution.py:489
  26.6 1.0 copy-start.1
  27.6 1.0 copy-start.2
  28.6 1.0 copy-start.3
  29.6 0.9 copy-start.4
  30.5 0.9 copy-start.5
  31.4 33.0 %copy-start.8 = (bf16[3,256,384]{2,1,0:T(8,128)(2,1)S(1)}, bf16[3,256,384]{2,1,0:T(8,128)(2,1)}, u32[]{:S(2)}) copy-start(bf16[3,256,384]{2,1,0:T(8,128)(2,1)} %lat_ref.1) | copy-start | bytes 1769476
  62.7 0.9 copy-start.6
  63.7 0.7 copy-start.10
  64.4 1.2 copy-start.7
  65.6 1.1 copy-start.9
  66.7 1.0 copy-start.11
  100.4 2.0 %copy-start = (bf16[4,1152,384]{2,1,0:T(8,128)(2,1)S(1)}, bf16[4,1152,384]{2,1,0:T(8,128)(2,1)}, u32[]{:S(2)}) copy-start(bf16[4,1152,384]{2,1,0:T(8,128)(2,1)} %get-tuple-element.37.pg) | copy-start | bytes 10616836
Sparse Core Ops, SparseCore 0:
  64.5 33.7 all-gather.1

commit v2 on v1

--- a/solution.py
+++ b/solution.py
@@ -12,6 +12,7 @@
 HD = 64
 D = 384
 TILES = 12
+PIECES = 3
 EPS = 1e-06
 GELU_C = 0.7978845608028654
 MESH = pl.DeviceIdType.MESH
@@ -56,7 +57,7 @@
 def gather_kernel(
     n, w0, w1, w2, w3, wada, silu, bada, bias,
     o0, o1, o2, o3, omod, obias,
-    silu_buf, mod_send, mod_buf, bias_buf,
+    silu_buf, mod_send, mod_buf, bias_buf, l_sem,
     g_send, g_recv, f_send, f_recv, s_send, s_recv, m_send, m_recv, b_send, b_recv,
 ):
     me = lax.axis_index("shard")
@@ -89,9 +90,12 @@
             )
             cp.start()
             pushes[m, d] = cp
-    for w, o in mats:
+    locals_ = []
+    for m, (w, o) in enumerate(mats):
         rows = w.shape[0]
-        o[pl.ds(pl.multiple_of(me * rows, 16), rows), :] = w[...]
+        cp = pltpu.make_async_copy(w, o.at[pl.ds(pl.multiple_of(me * rows, 16), rows)], l_sem.at[m])
+        cp.start()
+        locals_.append(cp)
 
     silu_buf[me] = silu[me]
     for cp, _ in small:
@@ -132,7 +136,7 @@
             cp = remote(o.at[spot], o.at[spot], f_send.at[m, d], f_recv.at[m, d], sibling)
             cp.start()
             passed.append(cp)
-    for cp in passed:
+    for cp in passed + locals_:
         cp.wait()
     for cp in pushes.values():
         cp.wait_send()
@@ -146,32 +150,33 @@
 def gather_weights(n, w_qkv, w_out, w_up, w_down, w_ada, silu, bada, bias):
     mats = (w_qkv, w_out, w_up, w_down)
     vmem = pl.BlockSpec(memory_space=pltpu.VMEM)
+    hbm = pl.BlockSpec(memory_space=pl.ANY)
     dma = pltpu.SemaphoreType.DMA
     return pl.pallas_call(
         functools.partial(gather_kernel, n),
         out_shape=[jax.ShapeDtypeStruct((n * w.shape[0], w.shape[1]), BF16) for w in mats]
-        + [jax.ShapeDtypeStruct(bada.shape[:0] + (8, bada.shape[1]), F32), jax.ShapeDtypeStruct(bias.shape, F32)],
-        in_specs=[vmem] * 8,
-        out_specs=[vmem] * 6,
+        + [jax.ShapeDtypeStruct((8, bada.shape[1]), F32), jax.ShapeDtypeStruct(bias.shape, F32)],
+        in_specs=[hbm] * 4 + [vmem] * 4,
+        out_specs=[hbm] * 4 + [vmem] * 2,
         scratch_shapes=[
             pltpu.VMEM(silu.shape, BF16),
             pltpu.VMEM((n, 8, bada.shape[1]), F32),
             pltpu.VMEM((n, 8, bada.shape[1]), F32),
             pltpu.VMEM((n,) + bias.shape, F32),
-            dma((4, n)), dma((4, n)), dma((4, n)), dma((4, n)),
+            dma((4,)), dma((4, n)), dma((4, n)), dma((4, n)), dma((4, n)),
             dma((n,)), dma((n,)), dma((n,)), dma((n,)), dma((n,)), dma((n,)),
         ],
         compiler_params=pltpu.CompilerParams(
-            collective_id=0, has_side_effects=True, vmem_limit_bytes=32 * MIB
+            collective_id=0, has_side_effects=True, vmem_limit_bytes=58 * MIB
         ),
         name="gather_weights",
     )(*mats, w_ada, silu, bada, bias)
 
 
 def block_kernel(
-    lat_ref, cot_ref, mod_ref, bias_ref, wqkv, wout, wup, wdown,
-    out_ref, ing_ref, dmod_ref, pg_ref, gb_ref,
-    acc, proj_s, prob_s, heads_s, act_s, slope_s, dproj_s,
+    lat_ref, cot_ref, mod_ref, bias_ref, silu_ref, wqkv, wout, wup, wdown,
+    out_ref, ing_ref, dmod_ref, pg_ref, pay_ref,
+    gb_ref, dm_s, acc, proj_s, prob_s, heads_s, act_s, slope_s, dproj_s,
 ):
     step = pl.program_id(0)
     last = pl.num_programs(0) - 1
@@ -288,32 +293,47 @@
     g1 = dattn_in * (1.0 + scale1)
     ing_ref[0] = dmid + recip1 * (g1 - row(g1) - normed1 * row(g1 * normed1))
 
+    for j in range(6):
+        dm_s[pl.ds(step * 6 + j, 1), :] = dmod_ref[0, j : j + 1, :]
+
     @pl.when(step == last)
     def _():
+        batch = silu_ref.shape[0]
+        fill = pay_ref.shape[0] - 7 * batch - 8
+        pay_ref[...] = jnp.concatenate(
+            [dm_s[...], silu_ref[...], gb_ref[...], jnp.zeros((fill, D), F32)]
+        ).astype(BF16)
         for s in range(4):
             for t in range(8):
                 pg_ref[s, t * 96 : (t + 1) * 96, :] = acc[t, s * 96 : (s + 1) * 96, :].astype(BF16)
             pg_ref[s, 768:1152, :] = acc[8 + s].astype(BF16)
 
 
-def run_block(latents, cotangent, modul, bias, wqkv, wout, wup, wdown):
+def run_block(latents, cotangent, modul, bias, silu, wqkv, wout, wup, wdown):
     batch, length, width = latents.shape
     tok = pl.BlockSpec((1, length, width), lambda i: (i, 0, 0))
     mod = pl.BlockSpec((1, 6, width), lambda i: (i, 0, 0))
     whole = pl.BlockSpec(memory_space=pltpu.VMEM)
+    rows = 7 * batch + 8
+
+    def full(a):
+        return pl.BlockSpec(a.shape, lambda i: (0, 0))
+
     return pl.pallas_call(
         block_kernel,
         grid=(batch,),
-        in_specs=[tok, tok, mod] + [whole] * 5,
+        in_specs=[tok, tok, mod] + [full(a) for a in (bias, silu, wqkv, wout, wup, wdown)],
         out_specs=[tok, tok, mod, whole, whole],
         out_shape=[
             jax.ShapeDtypeStruct(latents.shape, F32),
             jax.ShapeDtypeStruct(latents.shape, F32),
             jax.ShapeDtypeStruct((batch, 6, width), F32),
             jax.ShapeDtypeStruct((4, 96 * TILES, width), BF16),
-            jax.ShapeDtypeStruct((8, width), F32),
+            jax.ShapeDtypeStruct((rows + -rows % 16, width), BF16),
         ],
         scratch_shapes=[
+            pltpu.VMEM((8, width), F32),
+            pltpu.VMEM((6 * batch, width), F32),
             pltpu.VMEM((TILES, D, D), F32),
             pltpu.VMEM((length, 3 * D), BF16),
             pltpu.VMEM((H, length, length), F32),
@@ -323,11 +343,11 @@
             pltpu.VMEM((length, 3 * D), BF16),
         ],
         compiler_params=pltpu.CompilerParams(
-            dimension_semantics=("arbitrary",), vmem_limit_bytes=48 * MIB
+            dimension_semantics=("arbitrary",), vmem_limit_bytes=58 * MIB
         ),
         cost_estimate=pl.CostEstimate(flops=9 * 10**9, bytes_accessed=12 * 10**6, transcendentals=2 * 10**6),
         name="block",
-    )(latents, cotangent, modul, bias, wqkv, wout, wup, wdown)
+    )(latents, cotangent, modul, bias, silu, wqkv, wout, wup, wdown)
 
 
 def reduce_kernel(
@@ -346,81 +366,99 @@
     zpeers = [(me, zs[d] * 2 + core) for d in range(1, nz)]
     barrier([sibling] + speers + zpeers)
     half = pg.shape[1] // 2
-    chunk = half // nz
-    own = pl.ds(pl.multiple_of(core * half, 16), half)
-    other = pl.ds(pl.multiple_of((1 - core) * half, 16), half)
+    piece = half // PIECES
+    chunk = piece // nz
 
     order = [1, 3, 2, 0] if n == 4 else list(range(1, n)) + [0]
-    firsts = {}
-    for d in order:
-        s = lax.rem(me + d, n)
-        cp = remote(pg.at[s, other], sib_buf.at[s], a_send.at[d], a_recv.at[d], sibling)
+    sent = []
+
+    def go(*args):
+        cp = remote(*args)
         cp.start()
-        firsts[d] = cp
-    pz = []
-    for d in range(1, nz):
-        cp = remote(pay, pays.at[core, me, z], pz_send.at[d], pz_recv.at[d], zpeers[d - 1])
-        cp.start()
-        pz.append(cp)
+        sent.append(cp)
+        return cp
+
+    def spot(side, c, off, size):
+        return pl.ds(pl.multiple_of(side * half + c * piece + off, 16), size)
+
+    firsts, seconds, thirds, fourths, fifths = {}, {}, {}, {}, []
+    for c in range(PIECES):
+        for d in order:
+            s = lax.rem(me + d, n)
+            firsts[c, d] = go(
+                pg.at[s, spot(1 - core, c, 0, piece)], sib_buf.at[c, s],
+                a_send.at[c, d], a_recv.at[c, d], sibling,
+            )
+    pz = [
+        go(pay, pays.at[core, me, z], pz_send.at[d], pz_recv.at[d], zpeers[d - 1])
+        for d in range(1, nz)
+    ]
     pays[core, me, z] = pay[...]
-    seconds = {}
-    for d in order:
-        s = lax.rem(me + d, n)
-        firsts[d].wait_recv()
-        both = pg[s, own, :].astype(F32) + sib_buf[s].astype(F32)
-        chip[s] = both.astype(BF16)
-        if d:
-            cp = remote(chip.at[s], grp_buf.at[me], b_send.at[d], b_recv.at[d], speers[d - 1])
-            cp.start()
-            seconds[d] = cp
+
+    def pair(c):
+        for d in order:
+            s = lax.rem(me + d, n)
+            firsts[c, d].wait_recv()
+            both = pg[s, spot(core, c, 0, piece), :].astype(F32) + sib_buf[c, s].astype(F32)
+            chip[c, s] = both.astype(BF16)
+            if d:
+                seconds[c, d] = go(
+                    chip.at[c, s], grp_buf.at[c, me], b_send.at[c, d], b_recv.at[c, d], speers[d - 1]
+                )
+
+    def group(c):
+        total = chip[c, me].astype(F32)
+        for d in range(1, n):
+            seconds[c, d].wait_recv()
+            total = total + grp_buf[c, lax.rem(me - d + n, n)].astype(F32)
+        mine[c] = total.astype(BF16)
+        for d in range(1, nz):
+            part = pl.ds(pl.multiple_of(zs[d] * chunk, 16), chunk)
+            thirds[c, d] = go(
+                mine.at[c, part], z_buf.at[c, z], c_send.at[c, d], c_recv.at[c, d], zpeers[d - 1]
+            )
+
+    def column(c):
+        total = mine[c, pl.ds(pl.multiple_of(z * chunk, 16), chunk), :].astype(F32)
+        for d in range(1, nz):
+            thirds[c, d].wait_recv()
+            total = total + z_buf[c, lax.rem(z - d + nz, nz)].astype(F32)
+        at = spot(core, c, z * chunk, chunk)
+        out[at, :] = total.astype(BF16)
+        for d in range(1, nz):
+            fourths[c, d] = go(
+                out.at[at], out.at[at], d_send.at[c, d], d_recv.at[c, d], zpeers[d - 1]
+            )
+        fifths.append(go(out.at[at], out.at[at], e_send.at[c, 0], e_recv.at[c, 0], sibling))
+
+    def share(c):
+        for d in range(1, nz):
+            fourths[c, d].wait_recv()
+            at = spot(core, c, lax.rem(z - d + nz, nz) * chunk, chunk)
+            fifths.append(go(out.at[at], out.at[at], e_send.at[c, d], e_recv.at[c, d], sibling))
+
+    for c in range(PIECES):
+        pair(c)
     for cp in pz:
         cp.wait_recv()
-    ps = []
-    for d in range(1, n):
-        cp = remote(pays.at[core, me], pays.at[core, me], ps_send.at[d], ps_recv.at[d], speers[d - 1])
-        cp.start()
-        ps.append(cp)
-    for d in range(1, n):
-        seconds[d].wait_recv()
-    total = chip[me].astype(F32)
-    for d in range(1, n):
-        total = total + grp_buf[lax.rem(me + d, n)].astype(F32)
-    mine[...] = total.astype(BF16)
-    thirds = []
-    for d in range(1, nz):
-        spot = pl.ds(pl.multiple_of(zs[d] * chunk, 16), chunk)
-        cp = remote(mine.at[spot], z_buf.at[z], c_send.at[d], c_recv.at[d], zpeers[d - 1])
-        cp.start()
-        thirds.append(cp)
+    group(0)
+    ps = [
+        go(pays.at[core, me], pays.at[core, me], ps_send.at[d], ps_recv.at[d], speers[d - 1])
+        for d in range(1, n)
+    ]
+    for c in range(1, PIECES):
+        group(c)
+        column(c - 1)
     for cp in ps:
         cp.wait_recv()
-    pc = remote(pays.at[core], pays.at[core], pc_send, pc_recv, sibling)
-    pc.start()
-    for cp in thirds:
+    pc = go(pays.at[core], pays.at[core], pc_send, pc_recv, sibling)
+    column(PIECES - 1)
+    for c in range(PIECES):
+        share(c)
+    for cp in fifths:
         cp.wait_recv()
-    total = mine[pl.ds(pl.multiple_of(z * chunk, 16), chunk), :].astype(F32)
-    for d in range(1, nz):
-        total = total + z_buf[zs[d]].astype(F32)
-    spot = pl.ds(pl.multiple_of(core * half + z * chunk, 16), chunk)
-    out[spot, :] = total.astype(BF16)
-    fourths = []
-    for d in range(1, nz):
-        cp = remote(out.at[spot], out.at[spot], d_send.at[d], d_recv.at[d], zpeers[d - 1])
-        cp.start()
-        fourths.append(cp)
-    fifths = [remote(out.at[spot], out.at[spot], e_send.at[0], e_recv.at[0], sibling)]
-    fifths[0].start()
-    for d in range(1, nz):
-        fourths[d - 1].wait_recv()
-        origin = lax.rem(z - d + nz, nz)
-        spot = pl.ds(pl.multiple_of(core * half + origin * chunk, 16), chunk)
-        cp = remote(out.at[spot], out.at[spot], e_send.at[d], e_recv.at[d], sibling)
-        cp.start()
-        fifths.append(cp)
-    for cp in fifths:
-        cp.wait()
-    pc.wait()
-    for cp in list(firsts.values()) + list(seconds.values()) + thirds + fourths + pz + ps:
+    pc.wait_recv()
+    for cp in sent:
         cp.wait_send()
 
 
@@ -428,7 +466,7 @@
     vmem = pl.BlockSpec(memory_space=pltpu.VMEM)
     dma = pltpu.SemaphoreType.DMA
     rows, width = pg.shape[1:]
-    half = rows // 2
+    piece = rows // 2 // PIECES
     return pl.pallas_call(
         functools.partial(reduce_kernel, n, nz),
         out_shape=[
@@ -438,25 +476,162 @@
         in_specs=[vmem] * 2,
         out_specs=[vmem] * 2,
         scratch_shapes=[
-            pltpu.VMEM((n, half, width), BF16),
-            pltpu.VMEM((n, half, width), BF16),
-            pltpu.VMEM((n, half, width), BF16),
-            pltpu.VMEM((half, width), BF16),
-            pltpu.VMEM((nz, half // nz, width), BF16),
-            dma((n,)), dma((n,)), dma((n,)), dma((n,)),
-            dma((nz,)), dma((nz,)), dma((nz,)), dma((nz,)), dma((nz,)), dma((nz,)),
+            pltpu.VMEM((PIECES, n, piece, width), BF16),
+            pltpu.VMEM((PIECES, n, piece, width), BF16),
+            pltpu.VMEM((PIECES, n, piece, width), BF16),
+            pltpu.VMEM((PIECES, piece, width), BF16),
+            pltpu.VMEM((PIECES, nz, piece // nz, width), BF16),
+            dma((PIECES, n)), dma((PIECES, n)), dma((PIECES, n)), dma((PIECES, n)),
+            dma((PIECES, nz)), dma((PIECES, nz)), dma((PIECES, nz)),
+            dma((PIECES, nz)), dma((PIECES, nz)), dma((PIECES, nz)),
             dma((nz,)), dma((nz,)), dma((n,)), dma((n,)), dma, dma,
         ],
         compiler_params=pltpu.CompilerParams(
-            collective_id=1, has_side_effects=True, vmem_limit_bytes=40 * MIB
+            collective_id=1, has_side_effects=True, vmem_limit_bytes=58 * MIB
         ),
         name="reduce_grads",
     )(pg, pay)
 
 
-def place(piece, n, me):
-    full = jnp.zeros((n * piece.shape[0],), F32)
-    return lax.dynamic_update_slice(full, piece.astype(F32), (me * piece.shape[0],))
+def prep_kernel(
+    n, steps, labels, time_table, class_table, b_ada, b_qv, b_out, b_up, b_down,
+    cond_ref, silu_ref, blocks_ref, bada_ref, bias_ref, rows, sems,
+):
+    me = lax.axis_index("shard")
+    batch, width = cond_ref.shape
+    copies = []
+    for i in range(batch):
+        for k, (table, index) in enumerate(((time_table, steps), (class_table, labels))):
+            cp = pltpu.make_async_copy(
+                table.at[pl.ds(index[i], 1)], rows.at[k, i], sems.at[k, i]
+            )
+            cp.start()
+            copies.append(cp)
+
+    def placed(value, s, total):
+        size = value.shape[1]
+        parts = [value.astype(F32)]
+        if s:
+            parts = [jnp.zeros((1, s * size), F32)] + parts
+        if (s + 1) * size < total:
+            parts = parts + [jnp.zeros((1, total - (s + 1) * size), F32)]
+        return jnp.concatenate(parts, axis=1) if len(parts) > 1 else parts[0]
+
+    for s in range(n):
+        @pl.when(me == s)
+        def _(s=s):
+            bada_ref[...] = placed(b_ada[...], s, 6 * width)
+            qv = placed(b_qv[...], s, 2 * width)
+            up = placed(b_up[...], s, 4 * width)
+            bias_ref[0:1, :] = qv[:, :width]
+            bias_ref[1:2, :] = qv[:, width:]
+            bias_ref[2:3, :] = placed(b_out[...], s, width)
+            for j in range(4):
+                bias_ref[3 + j : 4 + j, :] = up[:, j * width : (j + 1) * width]
+            bias_ref[7:8, :] = placed(b_down[...], s, width)
+
+    for cp in copies:
+        cp.wait()
+    cond = jnp.concatenate([rows[0, i] + rows[1, i] for i in range(batch)])
+    cond_ref[...] = cond
+    silu = cond * jax.nn.sigmoid(cond)
+    silu_ref[...] = silu
+    share = width // n
+    padded = jnp.concatenate([silu, jnp.zeros((16 - batch, width), F32)])
+    for p in range(n):
+        blocks_ref[p] = padded[:, p * share : (p + 1) * share].astype(BF16)
+
+
+def prepare(n, timesteps, labels, time_table, class_table, biases):
+    batch, width = timesteps.shape[0], time_table.shape[1]
+    vmem = pl.BlockSpec(memory_space=pltpu.VMEM)
+    hbm = pl.BlockSpec(memory_space=pl.ANY)
+    smem = pl.BlockSpec(memory_space=pltpu.SMEM)
+    return pl.pallas_call(
+        functools.partial(prep_kernel, n),
+        out_shape=[
+            jax.ShapeDtypeStruct((batch, width), F32),
+            jax.ShapeDtypeStruct((batch, width), F32),
+            jax.ShapeDtypeStruct((n, 16, width // n), BF16),
+            jax.ShapeDtypeStruct((1, 6 * width), F32),
+            jax.ShapeDtypeStruct((8, width), F32),
+        ],
+        in_specs=[smem] * 2 + [hbm] * 2 + [vmem] * 5,
+        out_specs=[vmem] * 5,
+        scratch_shapes=[
+            pltpu.VMEM((2, batch, 1, width), F32),
+            pltpu.SemaphoreType.DMA((2, batch)),
+        ],
+        compiler_params=pltpu.CompilerParams(vmem_limit_bytes=58 * MIB),
+        name="prepare",
+    )(timesteps, labels, time_table, class_table, *[b[None, :] for b in biases])
+
+
+def finish_kernel(
+    n, batch, own, pays, w_ada, dmod, cond_ref,
+    cond_grad, g_ada, gb_ada, g_qkv, gb_qv, g_out, gb_out, g_up, gb_up, g_down, gb_down, wide,
+):
+    me = lax.axis_index("shard")
+    for t in range(3):
+        g_qkv[:, t * D : (t + 1) * D] = own[t * 96 : (t + 1) * 96, :].astype(F32)
+    g_out[...] = own[288:384, :].astype(F32)
+    for t in range(4):
+        g_up[:, t * D : (t + 1) * D] = own[(4 + t) * 96 : (5 + t) * 96, :].astype(F32)
+    g_down[...] = own[768:, :].astype(F32)
+
+    share = D // n
+    rows_of = pl.ds(pl.multiple_of(me * share, 8), share)
+    silu = jnp.concatenate([pays[6 * batch + i] for i in range(batch)])
+    sums = []
+    for j in range(6):
+        dm = jnp.concatenate([pays[6 * i + j] for i in range(batch)])
+        wide[...] = mm_at(silu, dm)
+        g_ada[:, j * D : (j + 1) * D] = wide[rows_of, :]
+        sums.append(cols(dm.astype(F32)))
+    ada = jnp.concatenate(sums, axis=1)
+    gb = [cols(pays[7 * batch + i].astype(F32)) for i in range(8)]
+    qv = jnp.concatenate(gb[0:2], axis=1)
+    for s in range(n):
+        @pl.when(me == s)
+        def _(s=s):
+            def part(value):
+                size = value.shape[1] // n
+                return value[:, s * size : (s + 1) * size]
+
+            gb_ada[...] = part(ada)
+            gb_qv[...] = part(qv)
+            gb_out[...] = part(gb[2])
+            gb_up[...] = part(jnp.concatenate(gb[3:7], axis=1))
+            gb_down[...] = part(gb[7])
+
+    total = jnp.zeros((3 * batch, D), F32)
+    for j in range(6):
+        dm = jnp.concatenate([dmod[i, j : j + 1, :] for i in range(batch)])
+        high = dm.astype(BF16).astype(F32)
+        middle = (dm - high).astype(BF16).astype(F32)
+        low = dm - high - middle
+        three = jnp.concatenate([high, middle, low]).astype(BF16)
+        total = total + mm_bt(three, w_ada[:, j * D : (j + 1) * D])
+    cond = cond_ref[...]
+    sig = jax.nn.sigmoid(cond)
+    grad = total[:batch] + total[batch : 2 * batch] + total[2 * batch :]
+    cond_grad[...] = grad * (sig * (1.0 + cond * (1.0 - sig)))
+
+
+def finish(n, own, pays, w_ada, dmod, cond):
+    batch = cond.shape[0]
+    vmem = pl.BlockSpec(memory_space=pltpu.VMEM)
+    shapes = [(batch, D), (D // n, 6 * D), (1, 6 * D // n), (D // n, 3 * D), (1, 2 * D // n), (D // n, D)]
+    shapes += [(1, D // n), (D // n, 4 * D), (1, 4 * D // n), (4 * D // n, D), (1, D // n)]
+    return pl.pallas_call(
+        functools.partial(finish_kernel, n, batch),
+        out_shape=[jax.ShapeDtypeStruct(shape, F32) for shape in shapes],
+        in_specs=[vmem] * 5,
+        out_specs=[vmem] * 11,
+        scratch_shapes=[pltpu.VMEM((D, D), F32)],
+        compiler_params=pltpu.CompilerParams(vmem_limit_bytes=58 * MIB),
+        name="finish",
+    )(own, pays, w_ada, dmod, cond)
 
 
 def body(
@@ -464,80 +639,28 @@
     latents, cotangent, timesteps, labels, time_table, class_table,
     w_ada, b_ada, w_qkv, b_qv, w_out, b_out, w_up, b_up, w_down, b_down,
 ):
-    me = lax.axis_index("shard")
     batch, length, width = latents.shape
-    cond = jnp.concatenate(
-        [
-            lax.dynamic_slice(time_table, (timesteps[i], 0), (1, width))
-            + lax.dynamic_slice(class_table, (labels[i], 0), (1, width))
-            for i in range(batch)
-        ]
+    cond, silu, blocks, bada, bias = prepare(
+        n, timesteps, labels, time_table, class_table, (b_ada, b_qv, b_out, b_up, b_down)
     )
-    sig = jax.nn.sigmoid(cond)
-    silu_b = (cond * sig).astype(BF16)
-    share = width // n
-    silu = jnp.pad(
-        silu_b.reshape(batch, n, share).transpose(1, 0, 2), ((0, 0), (0, 16 - batch), (0, 0))
-    )
-    bias = jnp.concatenate(
-        [place(b_qv, n, me), place(b_out, n, me), place(b_up, n, me), place(b_down, n, me)]
-    ).reshape(8, width)
     wqkv, wout, wup, wdown, modul, bias = gather_weights(
-        n, w_qkv, w_out, w_up, w_down, w_ada, silu, place(b_ada, n, me)[None, :], bias
+        n, w_qkv, w_out, w_up, w_down, w_ada, blocks, bada, bias
     )
     w_late, _ = lax.optimization_barrier((w_ada, modul))
     w_ada_full = lax.all_gather(w_late, "shard", axis=0, tiled=True)
-    block_out, input_grad, dmod, pg, gb = run_block(
-        latents, cotangent, modul[:batch].reshape(batch, 6, width), bias, wqkv, wout, wup, wdown
+    block_out, input_grad, dmod, pg, pay = run_block(
+        latents, cotangent, modul[:batch].reshape(batch, 6, width), bias, silu, wqkv, wout, wup, wdown
     )
-    cond_grad = jnp.dot(
-        dmod.reshape(batch, 6 * width), w_ada_full.astype(F32).T, precision=lax.Precision.HIGHEST
-    ) * (sig * (1.0 + cond * (1.0 - sig)))
-
-    used = batch * 7 + 8
-    pay = jnp.concatenate(
-        [
-            dmod.reshape(batch * 6, width),
-            silu_b.astype(F32),
-            gb,
-            jnp.zeros((-used % 16, width), F32),
-        ]
-    ).astype(BF16)
     nz = reps // 2
-    if reps % 2 == 0 and pg.shape[1] % (32 * nz) == 0:
+    if reps % 2 == 0 and pg.shape[1] % (32 * PIECES * nz) == 0:
         own, pays = reduce_grads(n, nz, pg, pay)
-        own = own.astype(F32)
     else:
         own = lax.psum(lax.psum_scatter(pg.astype(F32), "shard", scatter_dimension=0), "rep")
         pays = lax.all_gather(pay, ("shard", "rep"))
-    pays = pays.reshape((-1,) + pay.shape)
-    count = pays.shape[0] * batch
-    dm = pays[:, : batch * 6].reshape(count, 6 * width)
-    silu_all = pays[:, batch * 6 : batch * 7].reshape(count, width)
-    silu_own = lax.dynamic_slice(silu_all, (0, me * share), (count, share))
-    grad_w_ada = mm_at(silu_own, dm)
-    grad_b_ada = jnp.sum(dm.astype(F32), axis=0)
-    gbs = jnp.sum(pays[:, batch * 7 : used].astype(F32), axis=0).reshape(-1)
-
-    def take(vec):
-        size = vec.shape[0] // n
-        return lax.dynamic_slice(vec, (me * size,), (size,))
-
-    tiles = [own[t * 96 : (t + 1) * 96] for t in range(8)]
-    return (
-        block_out,
-        input_grad,
-        cond_grad,
-        grad_w_ada,
-        take(grad_b_ada),
-        jnp.concatenate(tiles[0:3], axis=1),
-        take(gbs[: 2 * width]),
-        tiles[3],
-        take(gbs[2 * width : 3 * width]),
-        jnp.concatenate(tiles[4:8], axis=1),
-        take(gbs[3 * width : 7 * width]),
-        own[768:],
-        take(gbs[7 * width :]),
+    pays = pays.reshape((-1,) + pay.shape).transpose(1, 0, 2)
+    cond_grad, *grads = finish(n, own, pays, w_ada_full, dmod, cond)
+    return (block_out, input_grad, cond_grad) + tuple(
+        g.reshape(-1) if i % 2 else g for i, g in enumerate(grads)
     )
 
 

time: 171 us -> 142 us (0.83); the launches traced: 169 us -> 142 us
  local copies, waits for them, and re-layouts: 20.3 us -> 7.53 us
  between operations: 25.9 us -> 14.1 us
  Pallas kernels: 112 us -> 118 us
  matrix products: 4.86 us -> 0 us
  other arithmetic: 5.78 us -> 2.54 us
    unnamed x25 -> x0, local copies, waits for them, and re-layouts: 11.6 us -> none
    pallas_call x1 -> x3, Pallas kernels: 32.5 us -> 41.7 us  [the longest x1 34.8 us: run_block(): pl.pallas_call(block_kernel, grid=(batch,), in_specs=[tok, tok, mod] + [f...]
    pallas_call x1, Pallas kernels: 47.7 us -> 41.8 us  [reduce_grads(): pl.pallas_call(functools.partial(reduce_kernel, n, nz), out_shape=[jax.Sh...]
    dot_general x2 -> x0, matrix products: 4.86 us -> none  [the longest x1 3.57 us: body(): jnp.dot(dmod.reshape(batch, 6 * width), w_ada_full.astype(F32).T, precisi...]
    slice x11 -> x0, local copies, waits for them, and re-layouts: 4.45 us -> none  [the longest x1 1.35 us: body(): labels[i]]
    broadcast_in_dim x5 -> x3, local copies, waits for them, and re-layouts: 0.7 us -> 3.72 us  [prepare(): b[None, :]]
    pallas_call x1, Pallas kernels: 31.3 us -> 34.4 us  [gather_weights(): pl.pallas_call(functools.partial(gather_kernel, n), out_shape=[jax.ShapeD...]
    dynamic_update_slice x4 -> x0, other arithmetic: 2.99 us -> none  [place(): lax.dynamic_update_slice(full, piece.astype(F32), (me * piece.shape[0],))]
  transfers between devices with their start and end apart: 1 -> 1, of which waited for: 0 -> 0; matrix products, arithmetic and copies ran while one was open for 5% -> 3% of each run, Pallas kernels for 48% -> 54%
where the time goes in v2:
time: 142 us
  Pallas kernels  118 us (83%)
  between operations  14.1 us (10%)
  local copies, waits for them, and re-layouts  7.53 us (5%)
  other arithmetic  2.54 us (2%)
    pallas_call x1, Pallas kernels, reduce_grads(): pl.pallas_call(functools.partial(reduce_kernel, n, nz), out_shape=[jax.Sh...  41.8 us
    pallas_call x1, Pallas kernels, run_block(): pl.pallas_call(block_kernel, grid=(batch,), in_specs=[tok, tok, mod] + [f...  34.8 us
    pallas_call x1, Pallas kernels, gather_weights(): pl.pallas_call(functools.partial(gather_kernel, n), out_shape=[jax.ShapeD...  34.4 us
    pallas_call x1, Pallas kernels, finish(): pl.pallas_call(functools.partial(finish_kernel, n, batch), out_shape=[jax...  4.64 us
    broadcast_in_dim x3, local copies, waits for them, and re-layouts, prepare(): b[None, :]  3.72 us
  transfers between devices with their start and end apart: 1, of which 0 were waited for; matrix products, arithmetic and copies ran while one was open for 3% of the time, Pallas kernels for 54%

profile of v2, /device:TPU:0, one launch (start us, length us, event | category | flops | bytes accessed | tf_op | source)
XLA Modules:
  0.0 142.0 jit_solution(12194348080845958795)
XLA Ops:
  7.2 0.0 all-gather.2.cloned.1.call-start
  7.2 1.3 broadcast_in_dim.15.b_ada
  8.5 1.2 broadcast_in_dim.18.b_up
  9.7 1.2 broadcast_in_dim.16.b_qv
  11.0 2.3 %prepare.1 = (f32[3,384]{1,0:T(4,128)}, f32[3,384]{1,0:T(4,128)}, bf16[4,16,96]{2,1,0:T(8,128)(2,1)}, f32[1,2304]{1,0:T(1,128)}, f32[8,384]{1,0:T(8,128)}) custom-call(s32[3]{0:T(128)} %steps.1, s32[3]{0:T(128)} %labels.1, f32[1000,384]{1,0:T(8,128)} %time_table.1, f32[1001,384]{1,0:T(8,128)} %class_table.1, bf16[1,576]{1,0:T(2,128)(2,1)} %broadcast_in_dim.15.b_ada, ...), custom_call_target="tpu_custom_call" | custom-call | tf_op jit(solution)/shard_map/prepare/pallas_call | solution.py:550
  13.3 34.4 %gather_weights.1 = (bf16[384,1152]{1,0:T(8,128)(2,1)}, bf16[384,384]{1,0:T(8,128)(2,1)}, bf16[384,1536]{1,0:T(8,128)(2,1)}, bf16[1536,384]{1,0:T(8,128)(2,1)}, f32[8,2304]{1,0:T(8,128)}, /*index=5*/f32[8,384]{1,0:T(8,128)}) custom-call(bf16[96,1152]{1,0:T(8,128)(2,1)} %w0.1, bf16[96,384]{1,0:T(8,128)(2,1)} %w1.1, bf16[96,1536]{1,0:T(8,128)(2,1)} %w2.1, ...), custom_call_target="tpu_custom_call" | custom-call | tf_op jit(solution)/shard_map/gather_weights/pallas_call | solution.py:155
  47.6 0.0 all-gather.2.cloned.1.call-update
  47.7 0.9 slice.3
  48.6 0.6 reshape.47.mod_ref
  49.2 34.8 %block.1 = (f32[3,256,384]{2,1,0:T(8,128)}, f32[3,256,384]{2,1,0:T(8,128)}, f32[3,6,384]{2,1,0:T(8,128)}, bf16[4,1152,384]{2,1,0:T(8,128)(2,1)}, bf16[32,384]{1,0:T(8,128)(2,1)}) custom-call(bf16[3,256,384]{2,1,0:T(8,128)(2,1)} %lat_ref.1, bf16[3,256,384]{2,1,0:T(8,128)(2,1)} %cot_ref.1, f32[3,6,384]{2,1,0:T(8,128)} %reshape.47.mod_ref, ...), custom_call_target="tpu_custom_call" | custom-call | flops 8999999488 | bytes 12000000 | tf_op jit(solution)/shard_map/block/pallas_call | solution.py:322
  84.0 41.8 %reduce_grads.1 = (bf16[1152,384]{1,0:T(8,128)(2,1)}, bf16[2,4,4,32,384]{4,3,2,1,0:T(8,128)(2,1)}) custom-call(bf16[4,1152,384]{2,1,0:T(8,128)(2,1)} %get-tuple-element.55.pg, bf16[32,384]{1,0:T(8,128)(2,1)} %get-tuple-element.56.pay), custom_call_target="tpu_custom_call" | custom-call | tf_op jit(solution)/shard_map/reduce_grads/pallas_call | solution.py:470
  125.7 2.3 %copy.32 = bf16[32,32,384]{2,0,1:T(8,128)(2,1)} copy(bf16[32,32,384]{2,1,0:T(8,128)(2,1)} %bitcast.10) | data formatting | bytes 1572864 | tf_op jit(solution)/shard_map/reshape | solution.py:660
  128.0 0.0 all-gather.2.cloned.1.call-done.w_ada
  128.0 4.6 %finish.1 = (f32[3,384]{1,0:T(4,128)}, f32[96,2304]{1,0:T(8,128)}, f32[1,576]{1,0:T(1,128)}, f32[96,1152]{1,0:T(8,128)}, f32[1,192]{1,0:T(1,128)}, /*index=5*/f3...) custom-call(bf16[1152,384]{1,0:T(8,128)(2,1)} %get-tuple-element.57., ...), custom_call_target="tpu_custom_call" | custom-call | tf_op jit(solution)/shard_map/finish/pallas_call | solution.py:626
  132.7 1.3 reduce
  133.9 1.3 reduce.1
Async XLA Ops:
  7.2 120.8 %all-gather.2.cloned.1.call-start = ((), (), s32[]{:S(2)}) async-start(), calls=%async_computation | async-start | bytes 2211840 | tf_op jit(solution)/shard_map/all_gather | solution.py:650
Sparse Core Ops, SparseCore 0:
  47.8 32.7 all-gather.1

commit v3 on v2

--- a/solution.py
+++ b/solution.py
@@ -77,19 +77,25 @@
         small.append((cp, bp))
 
     mats = [(w0, o0), (w1, o1), (w2, o2), (w3, o3)]
+    across = me + 1 - 2 * lax.rem(me, 2)
+    along = me + 2 - 4 * (me // 2)
+    first = across * (1 - core) + along * core
+    second = across * core + along * (1 - core)
+
+    def block(w, origin):
+        rows = w.shape[0]
+        return pl.ds(pl.multiple_of(origin * rows + core * (rows // 2), 16), rows // 2)
+
     pushes = {}
     for m, (w, o) in enumerate(mats):
-        rows = w.shape[0]
-        half = rows // 2
-        mine = pl.multiple_of(core * half, 16)
-        for d in (1, 3, 2) if n == 4 else range(1, n):
+        half = w.shape[0] // 2
+        mine = w.at[pl.ds(pl.multiple_of(core * half, 16), half)]
+        for k, peer in enumerate((first, second)):
             cp = remote(
-                w.at[pl.ds(mine, half)],
-                o.at[pl.ds(pl.multiple_of(me * rows + core * half, 16), half)],
-                g_send.at[m, d], g_recv.at[m, d], peers[d - 1],
+                mine, o.at[block(w, me)], g_send.at[m, k], g_recv.at[m, k], (peer, rep)
             )
             cp.start()
-            pushes[m, d] = cp
+            pushes[m, k] = cp
     locals_ = []
     for m, (w, o) in enumerate(mats):
         rows = w.shape[0]
@@ -97,6 +103,18 @@
         cp.start()
         locals_.append(cp)
 
+    def relay(m):
+        w, o = mats[m]
+        pushes[m, 0].wait_recv()
+        at = block(w, first)
+        cp = remote(o.at[at], o.at[at], g_send.at[m, 2], g_recv.at[m, 2], (second, rep))
+        cp.start()
+        pushes[m, 2] = cp
+        cp = remote(o.at[at], o.at[at], f_send.at[m, 0], f_recv.at[m, 0], sibling)
+        cp.start()
+        passed.append(cp)
+
+    passed = []
     silu_buf[me] = silu[me]
     for cp, _ in small:
         cp.wait_recv()
@@ -105,12 +123,16 @@
     for p in range(n):
         mod_send[p] = part[p * 16 : p * 16 + 8] + bada_v
     mods = []
+    relay(0)
+    relay(1)
     for d in range(1, n):
         peer = peers[d - 1]
         cp = remote(mod_send.at[peer[0]], mod_buf.at[me], m_send.at[d], m_recv.at[d], peer)
         cp.start()
         mods.append(cp)
     mod_buf[me] = mod_send[me]
+    relay(2)
+    relay(3)
     bias_buf[me] = bias[...]
     for _, bp in small:
         bp.wait_recv()
@@ -125,17 +147,19 @@
         total = total + mod_buf[p]
     omod[...] = total
 
-    passed = []
-    for m, (w, o) in enumerate(mats):
-        rows = w.shape[0]
-        half = rows // 2
-        for d in (1, 3, 2) if n == 4 else range(1, n):
-            pushes[m, d].wait_recv()
-            origin = lax.rem(me - d + n, n)
-            spot = pl.ds(pl.multiple_of(origin * rows + core * half, 16), half)
-            cp = remote(o.at[spot], o.at[spot], f_send.at[m, d], f_recv.at[m, d], sibling)
-            cp.start()
-            passed.append(cp)
+
+    def hand(m, k, origin):
+        w, o = mats[m]
+        pushes[m, k].wait_recv()
+        at = block(w, origin)
+        cp = remote(o.at[at], o.at[at], f_send.at[m, k], f_recv.at[m, k], sibling)
+        cp.start()
+        passed.append(cp)
+
+    for m in range(4):
+        hand(m, 1, second)
+    for m in range(4):
+        hand(m, 2, 3 - me)
     for cp in passed + locals_:
         cp.wait()
     for cp in pushes.values():
@@ -520,15 +544,15 @@
     for s in range(n):
         @pl.when(me == s)
         def _(s=s):
-            bada_ref[...] = placed(b_ada[...], s, 6 * width)
-            qv = placed(b_qv[...], s, 2 * width)
-            up = placed(b_up[...], s, 4 * width)
+            bada_ref[...] = placed(b_ada[...].astype(F32).reshape(1, -1), s, 6 * width)
+            qv = placed(b_qv[...].astype(F32).reshape(1, -1), s, 2 * width)
+            up = placed(b_up[...].astype(F32).reshape(1, -1), s, 4 * width)
             bias_ref[0:1, :] = qv[:, :width]
             bias_ref[1:2, :] = qv[:, width:]
-            bias_ref[2:3, :] = placed(b_out[...], s, width)
+            bias_ref[2:3, :] = placed(b_out[...].astype(F32).reshape(1, -1), s, width)
             for j in range(4):
                 bias_ref[3 + j : 4 + j, :] = up[:, j * width : (j + 1) * width]
-            bias_ref[7:8, :] = placed(b_down[...], s, width)
+            bias_ref[7:8, :] = placed(b_down[...].astype(F32).reshape(1, -1), s, width)
 
     for cp in copies:
         cp.wait()
@@ -564,7 +588,7 @@
         ],
         compiler_params=pltpu.CompilerParams(vmem_limit_bytes=58 * MIB),
         name="prepare",
-    )(timesteps, labels, time_table, class_table, *[b[None, :] for b in biases])
+    )(timesteps, labels, time_table, class_table, *biases)
 
 
 def finish_kernel(
@@ -598,11 +622,11 @@
                 size = value.shape[1] // n
                 return value[:, s * size : (s + 1) * size]
 
-            gb_ada[...] = part(ada)
-            gb_qv[...] = part(qv)
-            gb_out[...] = part(gb[2])
-            gb_up[...] = part(jnp.concatenate(gb[3:7], axis=1))
-            gb_down[...] = part(gb[7])
+            gb_ada[...] = part(ada)[0]
+            gb_qv[...] = part(qv)[0]
+            gb_out[...] = part(gb[2])[0]
+            gb_up[...] = part(jnp.concatenate(gb[3:7], axis=1))[0]
+            gb_down[...] = part(gb[7])[0]
 
     total = jnp.zeros((3 * batch, D), F32)
     for j in range(6):
@@ -621,8 +645,8 @@
 def finish(n, own, pays, w_ada, dmod, cond):
     batch = cond.shape[0]
     vmem = pl.BlockSpec(memory_space=pltpu.VMEM)
-    shapes = [(batch, D), (D // n, 6 * D), (1, 6 * D // n), (D // n, 3 * D), (1, 2 * D // n), (D // n, D)]
-    shapes += [(1, D // n), (D // n, 4 * D), (1, 4 * D // n), (4 * D // n, D), (1, D // n)]
+    shapes = [(batch, D), (D // n, 6 * D), (6 * D // n,), (D // n, 3 * D), (2 * D // n,), (D // n, D)]
+    shapes += [(D // n,), (D // n, 4 * D), (4 * D // n,), (4 * D // n, D), (D // n,)]
     return pl.pallas_call(
         functools.partial(finish_kernel, n, batch),
         out_shape=[jax.ShapeDtypeStruct(shape, F32) for shape in shapes],
@@ -659,9 +683,7 @@
         pays = lax.all_gather(pay, ("shard", "rep"))
     pays = pays.reshape((-1,) + pay.shape).transpose(1, 0, 2)
     cond_grad, *grads = finish(n, own, pays, w_ada_full, dmod, cond)
-    return (block_out, input_grad, cond_grad) + tuple(
-        g.reshape(-1) if i % 2 else g for i, g in enumerate(grads)
-    )
+    return (block_out, input_grad, cond_grad) + tuple(grads)
 
 
 def solution(mesh):

time: 142 us -> 135 us (0.951)
  local copies, waits for them, and re-layouts: 7.53 us -> 3.8 us
  other arithmetic: 2.54 us -> 0 us
    broadcast_in_dim x3 -> x0, local copies, waits for them, and re-layouts: 3.72 us -> none  [prepare(): b[None, :]]
    pallas_call x2 -> x0, other arithmetic: 2.54 us -> none  [finish(): pl.pallas_call(functools.partial(finish_kernel, n, batch), out_shape=[jax...]
  transfers between devices with their start and end apart: 1 -> 1, of which waited for: 0 -> 0; matrix products, arithmetic and copies ran while one was open for 3% -> 3% of each run, Pallas kernels for 54% -> 56%
where the time goes in v3:
time: 135 us
  Pallas kernels  117 us (87%)
  between operations  14.1 us (10%)
  local copies, waits for them, and re-layouts  3.8 us (3%)
    pallas_call x1, Pallas kernels, reduce_grads(): pl.pallas_call(functools.partial(reduce_kernel, n, nz), out_shape=[jax.Sh...  41.2 us
    pallas_call x1, Pallas kernels, run_block(): pl.pallas_call(block_kernel, grid=(batch,), in_specs=[tok, tok, mod] + [f...  34.8 us
    pallas_call x1, Pallas kernels, gather_weights(): pl.pallas_call(functools.partial(gather_kernel, n), out_shape=[jax.ShapeD...  34.3 us
    pallas_call x1, Pallas kernels, finish(): pl.pallas_call(functools.partial(finish_kernel, n, batch), out_shape=[jax...  4.64 us
  transfers between devices with their start and end apart: 1, of which 0 were waited for; matrix products, arithmetic and copies ran while one was open for 3% of the time, Pallas kernels for 56%

profile of v3, /device:TPU:0, one launch (start us, length us, event | category | flops | bytes accessed | tf_op | source)
XLA Modules:
  0.0 135.2 jit_solution(1434616922282463595)
XLA Ops:
  7.2 0.0 all-gather.2.cloned.1.call-start
  7.2 2.3 %prepare.1 = (f32[3,384]{1,0:T(4,128)}, f32[3,384]{1,0:T(4,128)}, bf16[4,16,96]{2,1,0:T(8,128)(2,1)}, f32[1,2304]{1,0:T(1,128)}, f32[8,384]{1,0:T(8,128)}) custom-call(s32[3]{0:T(128)} %steps.1, s32[3]{0:T(128)} %labels.1, f32[1000,384]{1,0:T(8,128)} %time_table.1, f32[1001,384]{1,0:T(8,128)} %class_table.1, bf16[576]{0:T(1024)(128)(2,1)} %b_ada.1, ...), custom_call_target="tpu_custom_call" | custom-call | tf_op jit(solution)/shard_map/prepare/pallas_call | solution.py:574
  9.6 34.3 %gather_weights.1 = (bf16[384,1152]{1,0:T(8,128)(2,1)}, bf16[384,384]{1,0:T(8,128)(2,1)}, bf16[384,1536]{1,0:T(8,128)(2,1)}, bf16[1536,384]{1,0:T(8,128)(2,1)}, f32[8,2304]{1,0:T(8,128)}, /*index=5*/f32[8,384]{1,0:T(8,128)}) custom-call(bf16[96,1152]{1,0:T(8,128)(2,1)} %w0.1, bf16[96,384]{1,0:T(8,128)(2,1)} %w1.1, bf16[96,1536]{1,0:T(8,128)(2,1)} %w2.1, ...), custom_call_target="tpu_custom_call" | custom-call | tf_op jit(solution)/shard_map/gather_weights/pallas_call | solution.py:179
  43.9 0.0 all-gather.2.cloned.1.call-update
  43.9 0.9 slice.3
  44.8 0.6 reshape.32.mod_ref
  45.5 34.8 %block.1 = (f32[3,256,384]{2,1,0:T(8,128)}, f32[3,256,384]{2,1,0:T(8,128)}, f32[3,6,384]{2,1,0:T(8,128)}, bf16[4,1152,384]{2,1,0:T(8,128)(2,1)}, bf16[32,384]{1,0:T(8,128)(2,1)}) custom-call(bf16[3,256,384]{2,1,0:T(8,128)(2,1)} %lat_ref.1, bf16[3,256,384]{2,1,0:T(8,128)(2,1)} %cot_ref.1, f32[3,6,384]{2,1,0:T(8,128)} %reshape.32.mod_ref, ...), custom_call_target="tpu_custom_call" | custom-call | flops 8999999488 | bytes 12000000 | tf_op jit(solution)/shard_map/block/pallas_call | solution.py:346
  80.2 41.2 %reduce_grads.1 = (bf16[1152,384]{1,0:T(8,128)(2,1)}, bf16[2,4,4,32,384]{4,3,2,1,0:T(8,128)(2,1)}) custom-call(bf16[4,1152,384]{2,1,0:T(8,128)(2,1)} %get-tuple-element.55.pg, bf16[32,384]{1,0:T(8,128)(2,1)} %get-tuple-element.56.pay), custom_call_target="tpu_custom_call" | custom-call | tf_op jit(solution)/shard_map/reduce_grads/pallas_call | solution.py:494
  121.4 2.3 %copy.32 = bf16[32,32,384]{2,0,1:T(8,128)(2,1)} copy(bf16[32,32,384]{2,1,0:T(8,128)(2,1)} %bitcast.5) | data formatting | bytes 1572864 | tf_op jit(solution)/shard_map/reshape | solution.py:684
  123.7 0.0 all-gather.2.cloned.1.call-done.w_ada
  123.7 4.6 %finish.1 = (f32[3,384]{1,0:T(4,128)}, f32[96,2304]{1,0:T(8,128)}, f32[576]{0:T(1024)}, f32[96,1152]{1,0:T(8,128)}, f32[192]{0:T(256)}, /*index=5*/f32[96,384]{1...) custom-call(bf16[1152,384]{1,0:T(8,128)(2,1)} %get-tuple-element.57.own, ...), custom_call_target="tpu_custom_call" | custom-call | tf_op jit(solution)/shard_map/finish/pallas_call | solution.py:650
Async XLA Ops:
  7.2 116.5 %all-gather.2.cloned.1.call-start = ((), (), s32[]{:S(2)}) async-start(), calls=%async_computation | async-start | bytes 2211840 | tf_op jit(solution)/shard_map/all_gather | solution.py:674
Sparse Core Ops, SparseCore 0:
  44.1 31.9 all-gather.1
